TPU v7x, 128 devices: a whole 4x4x4 slice. The times are simulated.
128 devices in a mesh: row: 8 (over z, x_lo), col: 16 (over y, x_hi, core).
Axes of the slice: x: 4 (x_hi: 2, x_lo: 2; x = x_hi * 2 + x_lo), y: 4, z: 4, core: 2. Of those that a mesh axis runs over, the one named last changes fastest.
Arguments:
- emb_first: float32 [40, 32768], P(None, ('row', 'col')), may hold values from -6 to 6
- emb_second: float32 [40, 32768], P(None, ('row', 'col')), may hold values from -6 to 6
- signal: float32 [32, 32768], P(None, ('row', 'col')), may hold values from -6 to 6
- theta_first: float32 [40, 40], replicated, may hold values from -1 to 1
- theta_second: float32 [40, 40], replicated, may hold values from -1 to 1
- neighbors: int32 [20, 32768], P(None, 'row'), may hold values from 0 to 32767, as said below
- w_forward: float32 [96, 32], replicated, may hold values from -0.625 to 0.625
- w_backward: float32 [96, 32], replicated, may hold values from -0.625 to 0.625
Outputs:
- mixed: float32 [32, 32768], P(None, ('row', 'col'))
Inputs may be any that keep to these rules, and one draw needn't show every extreme that they name: For each node i the 20 entries neighbors[:, i] are distinct; entry k lies in the stretch of 32768 // 20 columns that begins k * (32768 // 20) columns after a start of its own for node i, counted cyclically over all 32768 columns.
All inputs are finite; a program needn't handle non-finite values.
Results may differ from a plain program's by a relative error of at most 0.00012.
Values sent between devices are 32-bit elements; how exact they have to be, the bound alone decides.
A program may use at most 128 MiB of HBM per device.

v0:
```python
import jax
import jax.numpy as jnp
from jax import lax
from jax.sharding import PartitionSpec as P

DEPTH = 2


keep_share = 0.05
tanh_scale = 3.0


def per_device(
    emb_first, emb_second, signal, theta_first, theta_second, neighbors, w_forward, w_backward
):
    highest = lax.Precision.HIGHEST
    row_count = lax.axis_size("row")
    col_count = lax.axis_size("col")
    row_index = lax.axis_index("row")
    col_index = lax.axis_index("col")
    block_nodes = signal.shape[1]
    row_nodes = block_nodes * col_count
    col_nodes = block_nodes * row_count
    emb_width = emb_first.shape[0]
    keep_count = neighbors.shape[0]
    m_first = jnp.tanh(
        tanh_scale
        * jnp.dot(theta_first.T, emb_first, precision=highest, preferred_element_type=jnp.float32)
    )
    m_second = jnp.tanh(
        tanh_scale
        * jnp.dot(theta_second.T, emb_second, precision=highest, preferred_element_type=jnp.float32)
    )
    home_data = jnp.concatenate([m_first, m_second, signal], axis=0)
    rows_all = lax.all_gather(home_data, "col", axis=1, tiled=True)
    gathered = lax.all_gather(rows_all, "row", axis=1, tiled=True)
    cols_all = lax.dynamic_slice_in_dim(gathered, col_index * col_nodes, col_nodes, 1)
    local_cols = neighbors - col_index * col_nodes
    col_iota = jnp.arange(col_nodes, dtype=jnp.int32)
    kept = jnp.zeros((row_nodes, col_nodes), jnp.float32)
    for slot_index in range(keep_count):
        kept = kept + (local_cols[slot_index][:, None] == col_iota[None, :]).astype(jnp.float32)
    left_side = jnp.concatenate([rows_all[:emb_width], rows_all[emb_width : 2 * emb_width]], axis=0)
    right_side = jnp.concatenate(
        [cols_all[emb_width : 2 * emb_width], -cols_all[:emb_width]], axis=0
    )
    score = lax.dot_general(
        left_side,
        right_side,
        (((0,), (0,)), ((), ())),
        precision=highest,
        preferred_element_type=jnp.float32,
    )
    tile = kept * jax.nn.relu(jnp.tanh(tanh_scale * score))
    degree_rows = 1.0 + lax.psum(jnp.sum(tile, axis=1), "col")
    degree_cols = 1.0 + lax.psum(jnp.sum(tile, axis=0), "row")
    signal_rows = rows_all[2 * emb_width :]
    signal_cols = cols_all[2 * emb_width :]
    fwd_list = [signal_rows]
    bwd_list = [signal_rows]
    fwd_cols, fwd_rows = (signal_cols, signal_rows)
    bwd_rows, bwd_cols = (signal_rows, signal_cols)
    for hop_index in range(DEPTH):
        forward_partial_sum = lax.dot_general(
            fwd_cols,
            tile,
            (((1,), (1,)), ((), ())),
            precision=highest,
            preferred_element_type=jnp.float32,
        )
        forward_summed = lax.psum(forward_partial_sum, "col")
        fwd_rows = (
            keep_share * signal_rows
            + (1.0 - keep_share) * (forward_summed + fwd_rows) / degree_rows[None, :]
        )
        fwd_list.append(fwd_rows)
        if hop_index + 1 < DEPTH:
            to_collected = lax.all_gather(fwd_rows, "row", axis=1, tiled=True)
            fwd_cols = lax.dynamic_slice_in_dim(to_collected, col_index * col_nodes, col_nodes, 1)
    for hop_index in range(DEPTH):
        partial_sum = jnp.dot(bwd_rows, tile, precision=highest, preferred_element_type=jnp.float32)
        summed = lax.psum(partial_sum, "row")
        bwd_cols = (
            keep_share * signal_cols
            + (1.0 - keep_share) * (summed + bwd_cols) / degree_cols[None, :]
        )
        collected = lax.all_gather(bwd_cols, "col", axis=1, tiled=True)
        bwd_rows = lax.dynamic_slice_in_dim(collected, row_index * row_nodes, row_nodes, 1)
        bwd_list.append(bwd_rows)
    home_start = col_index * block_nodes
    fwd_home = lax.dynamic_slice_in_dim(
        jnp.concatenate(fwd_list, axis=0), home_start, block_nodes, 1
    )
    bwd_home = lax.dynamic_slice_in_dim(
        jnp.concatenate(bwd_list, axis=0), home_start, block_nodes, 1
    )
    mixed = jnp.dot(w_forward.T, fwd_home, precision=highest, preferred_element_type=jnp.float32)
    mixed = mixed + jnp.dot(
        w_backward.T, bwd_home, precision=highest, preferred_element_type=jnp.float32
    )
    return mixed


def solution(mesh):
    placed = (
        P(None, ("row", "col")),
        P(None, ("row", "col")),
        P(None, ("row", "col")),
        P(),
        P(),
        P(None, "row"),
        P(),
        P(),
    )
    return jax.shard_map(
        per_device, mesh=mesh, in_specs=placed, out_specs=P(None, ("row", "col")), check_vma=False
    )
```

profile of v0, /device:TPU:1, one launch (start us, length us, event | category | flops | bytes accessed | tf_op | source)
XLA Modules:
  0.0 1137.9 jit_solution(14638571560812514954)
XLA Ops:
  6.5 0.0 copy-start
  6.5 0.0 all-gather.6.cloned.1.call-start
  6.5 0.8 copy-done
  7.3 1.0 fusion.2
  8.3 1.0 fusion.1
  9.3 1.4 pad_maximum_fusion
  10.7 0.0 all-gather.6.cloned.1.call-update
  10.8 0.0 all-gather.8.cloned.1.call-start
  10.8 49.5 %all-gather.6.cloned.1.call-done = f32[112,4096]{1,0:T(8,128)} async-done(((f32[112,256]{1,0:T(8,128)}), f32[112,4096]{1,0:T(8,128)}) %all-gather.6.cloned.1.call-update) | async-done | bytes 1835024 | tf_op jit(solution)/shard_map/all_gather | solution.py:35
  60.3 0.0 all-gather.8.cloned.1.call-update
  60.3 0.0 all-reduce.9.cloned.1.call-start
  60.4 1.0 broadcast_subtract_fusion
  61.4 0.3 fusion.29
  61.7 284.8 %all-gather.8.cloned.1.call-done = f32[112,32768]{1,0:T(8,128)} async-done(((f32[112,4096]{1,0:T(8,128)}), f32[112,32768]{1,0:T(8,128)}) %all-gather.8.cloned.1.call-update) | async-done | bytes 14680080 | tf_op jit(solution)/shard_map/all_gather | solution.py:36
  346.5 1.1 fusion.27
  347.6 0.0 copy-start.3
  347.6 117.8 %fusion.26 = (f32[2048]{0:T(1024)S(1)}, f32[4096]{0:T(1024)S(1)}, f32[4096,2048]{1,0:T(8,128)}) fusion(f32[40,2048]{1,0:T(8,128)S(1)} %get-tuple-element.8, f32[40,2048]{1,0:T(8,128)S(1)} %get-tuple-element.7, f32[112,4096]{1,0:T(8,128)} %all-gather.6.cloned.1.call-done, s32[4096]{0:T(1024)S(1)} %bitcast.34, s32[4096]{0:T(1024)S(1)} %bitcast.35, ...), kind=kOutput, calls=%fused_computation.64 | convolution fusion | flops 8590092288 | bytes 35872768 | tf_op jit(solution)/shard_map/dot_general | solution.py:47
  465.5 0.0 copy-done.3
  465.5 23.6 %fusion.24 = f32[32,2048]{1,0:T(8,128)} fusion(f32[4096,2048]{1,0:T(8,128)} %get-tuple-element.30, f32[112,4096]{1,0:T(8,128)S(1)} %copy-done.3), kind=kOutput, calls=%fused_computation.62 | convolution fusion | flops 3221225472 | bytes 34340864 | tf_op jit(solution)/shard_map/dot_general | solution.py:81
  489.0 0.0 all-reduce.9.cloned.1.call-update
  489.1 0.0 all-reduce.5.cloned.1.call-start
  489.1 36.4 %fusion.9 = f32[32,4096]{1,0:T(8,128)} fusion(f32[4096,2048]{1,0:T(8,128)} %get-tuple-element.30, f32[112,32768]{1,0:T(8,128)} %all-gather.8.cloned.1.call-done, s32[]{:T(128)S(6)} %add.159, s32[]{:T(128)S(6)} %select_n.12), kind=kOutput, calls=%fused_computation.43 | convolution fusion | flops 3221225472 | bytes 34340872 | tf_op jit(solution)/shard_map/dot_general | solution.py:64
  525.5 15.2 %psum.46 = f32[2048]{0:T(1024)S(1)} all-reduce(f32[2048]{0:T(1024)S(1)} %get-tuple-element.5), channel_id=1, replica_groups=mesh['row'=8,'col'=16] {'row'}, use_global_device_ids=true, to_apply=%region_6.7 | all-reduce | flops 2048 | bytes 16384 | tf_op jit(solution)/shard_map/psum | solution.py:56
  540.8 0.0 all-reduce.5.cloned.1.call-update
  540.8 0.0 all-gather.12.cloned.1.call-start
  540.8 18.4 %all-reduce.9.cloned.1.call-done = f32[32,2048]{1,0:T(8,128)} async-done(((f32[32,2048]{1,0:T(8,128)}), f32[32,2048]{1,0:T(8,128)}) %all-reduce.9.cloned.1.call-update) | async-done | bytes 262160 | tf_op jit(solution)/shard_map/psum | solution.py:82
  559.3 1.8 divide_add_fusion.3
  561.1 0.0 all-gather.12.cloned.1.call-update
  561.1 0.0 all-gather.10.cloned.1.call-start
  561.1 65.0 %psum.43 = f32[4096]{0:T(1024)S(1)} all-reduce(f32[4096]{0:T(1024)S(1)} %get-tuple-element.6), channel_id=1, replica_groups=mesh['row'=8,'col'=16] {'col'}, use_global_device_ids=true, to_apply=%region_2.3 | all-reduce | flops 4096 | bytes 32768 | tf_op jit(solution)/shard_map/psum | solution.py:55
  626.2 78.3 %all-reduce.5.cloned.1.call-done = f32[32,4096]{1,0:T(8,128)} async-done(((f32[32,4096]{1,0:T(8,128)}), f32[32,4096]{1,0:T(8,128)}) %all-reduce.5.cloned.1.call-update) | async-done | bytes 524304 | tf_op jit(solution)/shard_map/psum | solution.py:71
  704.4 2.0 divide_add_fusion.1
  706.5 0.0 all-gather.10.cloned.1.call-update
  706.5 0.0 all-reduce.11.cloned.1.call-start
  706.5 57.0 %all-gather.12.cloned.1.call-done = f32[32,32768]{1,0:T(8,128)} async-done(((f32[32,2048]{1,0:T(8,128)}), f32[32,32768]{1,0:T(8,128)}) %all-gather.12.cloned.1.call-update) | async-done | bytes 4194320 | tf_op jit(solution)/shard_map/all_gather | solution.py:87
  763.5 0.0 copy-start.1
  763.5 1.1 constant_dynamic-slice_fusion.1
  764.6 0.0 copy-start.4
  764.6 0.0 copy-start.2
  764.6 0.0 copy-start.5
  764.6 0.0 copy-start.6
  764.7 34.7 %fusion.30 = f32[32,2048]{1,0:T(8,128)} fusion(f32[32,4096]{1,0:T(8,128)S(1)} %constant_dynamic-slice_fusion.1, f32[4096,2048]{1,0:T(8,128)} %get-tuple-element.30), kind=kOutput, calls=%fused_computation.68 | convolution fusion | flops 3221225472 | bytes 34340864 | tf_op jit(solution)/shard_map/dot_general | solution.py:81
  799.4 0.0 all-reduce.11.cloned.1.call-update
  799.4 0.0 all-reduce.7.cloned.1.call-start
  799.5 53.7 %all-gather.10.cloned.1.call-done = f32[32,32768]{1,0:T(8,128)} async-done(((f32[32,4096]{1,0:T(8,128)}), f32[32,32768]{1,0:T(8,128)}) %all-gather.10.cloned.1.call-update) | async-done | bytes 4194320 | tf_op jit(solution)/shard_map/all_gather | solution.py:78
  853.2 36.4 %fusion.7 = f32[32,4096]{1,0:T(8,128)} fusion(f32[4096,2048]{1,0:T(8,128)} %get-tuple-element.30, f32[32,32768]{1,0:T(8,128)} %all-gather.10.cloned.1.call-done, s32[]{:T(128)S(6)} %select_n.12), kind=kOutput, calls=%fused_computation.41 | convolution fusion | flops 3221225472 | bytes 34340868 | tf_op jit(solution)/shard_map/dot_general | solution.py:64
  889.6 0.0 all-reduce.7.cloned.1.call-update
  889.6 0.0 all-gather.14.cloned.1.call-start
  889.7 35.1 %all-reduce.11.cloned.1.call-done = f32[32,2048]{1,0:T(8,128)} async-done(((f32[32,2048]{1,0:T(8,128)}), f32[32,2048]{1,0:T(8,128)}) %all-reduce.11.cloned.1.call-update) | async-done | bytes 262160 | tf_op jit(solution)/shard_map/psum | solution.py:82
  924.7 0.0 copy-done.4
  924.7 1.8 divide_add_fusion.2
  926.6 0.0 all-gather.14.cloned.1.call-update
  926.6 143.4 %all-reduce.7.cloned.1.call-done = f32[32,4096]{1,0:T(8,128)} async-done(((f32[32,4096]{1,0:T(8,128)}), f32[32,4096]{1,0:T(8,128)}) %all-reduce.7.cloned.1.call-update) | async-done | bytes 524304 | tf_op jit(solution)/shard_map/psum | solution.py:71
  1070.0 0.0 copy-done.2
  1070.0 1.2 fusion.28
  1071.2 0.0 copy-done.5
  1071.2 0.2 fusion.16
  1071.4 57.8 %all-gather.14.cloned.1.call-done = f32[32,32768]{1,0:T(8,128)} async-done(((f32[32,2048]{1,0:T(8,128)}), f32[32,32768]{1,0:T(8,128)}) %all-gather.14.cloned.1.call-update) | async-done | bytes 4194320 | tf_op jit(solution)/shard_map/all_gather | solution.py:87
  1129.3 1.1 constant_dynamic-slice_fusion
  1130.3 0.0 copy-done.6
  1130.4 0.8 fusion.3
  1131.2 0.0 copy-done.1
  (3 shorter events, 0.0 us)
Async XLA Ops:
  6.5 0.8 copy-start
  6.5 53.8 %all-gather.6.cloned.1.call-start = ((), (), s32[]{:S(2)}) async-start(), calls=%async_computation | async-start | bytes 1949696 | tf_op jit(solution)/shard_map/all_gather | solution.py:35
  10.8 335.7 %all-gather.8.cloned.1.call-start = ((), (), s32[]{:S(2)}) async-start(), calls=%async_computation.1 | async-start | bytes 16515072 | tf_op jit(solution)/shard_map/all_gather | solution.py:36
  60.3 498.9 %all-reduce.9.cloned.1.call-start = ((), (), s32[]{:S(2)}) async-start(), calls=%async_computation.5 | async-start | bytes 524288 | tf_op jit(solution)/shard_map/psum | solution.py:82
  347.6 117.9 %copy-start.3 = (f32[112,4096]{1,0:T(8,128)S(1)}, f32[112,4096]{1,0:T(8,128)}, u32[]{:S(2)}) copy-start(f32[112,4096]{1,0:T(8,128)} %all-gather.6.cloned.1.call-done) | copy-start | bytes 5505028
  489.1 215.4 %all-reduce.5.cloned.1.call-start = ((), (), s32[]{:S(2)}) async-start(), calls=%async_computation.2 | async-start | bytes 1048576 | tf_op jit(solution)/shard_map/psum | solution.py:71
  540.8 222.7 %all-gather.12.cloned.1.call-start = ((), (), s32[]{:S(2)}) async-start(), calls=%async_computation.6 | async-start | bytes 4456448 | tf_op jit(solution)/shard_map/all_gather | solution.py:87
  561.1 292.1 %all-gather.10.cloned.1.call-start = ((), (), s32[]{:S(2)}) async-start(), calls=%async_computation.3 | async-start | bytes 4718592 | tf_op jit(solution)/shard_map/all_gather | solution.py:78
  706.5 218.3 %all-reduce.11.cloned.1.call-start = ((), (), s32[]{:S(2)}) async-start(), calls=%async_computation.7 | async-start | bytes 524288 | tf_op jit(solution)/shard_map/psum | solution.py:82
  763.5 367.6 %copy-start.1 = (f32[40,256]{1,0:T(8,128)S(1)}, f32[40,256]{1,0:T(8,128)}, u32[]{:S(2)}) copy-start(f32[40,256]{1,0:T(8,128)} %param.8) | copy-start | bytes 122884
  764.6 160.1 %copy-start.4 = (f32[32,2048]{1,0:T(8,128)S(1)}, f32[32,2048]{1,0:T(8,128)}, u32[]{:S(2)}) copy-start(f32[32,2048]{1,0:T(8,128)} %divide_add_fusion.3) | copy-start | bytes 786436
  764.6 305.4 %copy-start.2 = (f32[32,4096]{1,0:T(8,128)S(1)}, f32[32,4096]{1,0:T(8,128)}, u32[]{:S(2)}) copy-start(f32[32,4096]{1,0:T(8,128)} %divide_add_fusion.1) | copy-start | bytes 1572868
  764.6 306.6 %copy-start.5 = (f32[96,32]{0,1:T(8,128)S(1)}, f32[96,32]{0,1:T(8,128)}, u32[]{:S(2)}) copy-start(f32[96,32]{0,1:T(8,128)} %param.14) | copy-start | bytes 36868
  764.6 365.7 %copy-start.6 = (f32[96,32]{0,1:T(8,128)S(1)}, f32[96,32]{0,1:T(8,128)}, u32[]{:S(2)}) copy-start(f32[96,32]{0,1:T(8,128)} %param.15) | copy-start | bytes 36868
  799.4 270.6 %all-reduce.7.cloned.1.call-start = ((), (), s32[]{:S(2)}) async-start(), calls=%async_computation.4 | async-start | bytes 1048576 | tf_op jit(solution)/shard_map/psum | solution.py:71
  889.6 239.7 %all-gather.14.cloned.1.call-start = ((), (), s32[]{:S(2)}) async-start(), calls=%async_computation.8 | async-start | bytes 4456448 | tf_op jit(solution)/shard_map/all_gather | solution.py:87
Sparse Core Ops, SparseCore 0:
  10.9 49.3 all-gather.5
  61.9 284.5 all-gather.7
  489.2 70.0 all-reduce.8
  561.7 142.6 all-reduce.4
  706.7 56.7 all-gather.11
  765.0 88.1 all-gather.9
  855.7 69.0 all-reduce.10
  927.4 142.6 all-reduce.6
  1072.5 56.7 all-gather.13
where the time goes:
time: 1150 us; the launch traced here: 1140 us
  waiting for transfers between devices  778 us (68%)
  matrix products  252 us (22%)
  blocking collectives  80.2 us (7%)
  between operations  13.6 us (1%)
    all_gather x1, waiting for transfers between devices, per_device(): gathered = lax.all_gather(rows_all, 'row', axis=1, tiled=True)  285 us
    psum x2, waiting for transfers between devices, per_device(): forward_summed = lax.psum(forward_partial_sum, 'col')  222 us
    dot_general x1, matrix products, per_device(): lax.dot_general(left_side, right_side, (((0,), (0,)), ((), ())), precisio...  118 us
    all_gather x2, waiting for transfers between devices, per_device(): collected = lax.all_gather(bwd_cols, 'col', axis=1, tiled=True)  115 us
    dot_general x2, matrix products, per_device(): lax.dot_general(fwd_cols, tile, (((1,), (1,)), ((), ())), precision=highe...  72.8 us
    psum x1, blocking collectives, per_device(): degree_rows = 1.0 + lax.psum(jnp.sum(tile, axis=1), 'col')  65 us
    dot_general x2, matrix products, per_device(): jnp.dot(bwd_rows, tile, precision=highest, preferred_element_type=jnp.flo...  58.3 us
    all_gather x1, waiting for transfers between devices, per_device(): to_collected = lax.all_gather(fwd_rows, 'row', axis=1, tiled=True)  53.7 us
  transfers between devices with their start and end apart: 9, of which 9 were waited for; matrix products, arithmetic and copies ran while one was open for 10% of the time, Pallas kernels for 0%

commit v1 on v0

v1 whole, which is shorter than its diff:
```python
import jax
import jax.numpy as jnp
from jax import lax
from jax.experimental import pallas as pl
from jax.experimental.pallas import tpu as pltpu
from jax.sharding import PartitionSpec as P

KEEP = 0.05
GO = 1.0 - KEEP
HIGHEST = lax.Precision.HIGHEST
MESH = pl.DeviceIdType.MESH
f32, bf16, i32 = jnp.float32, jnp.bfloat16, jnp.int32

ROWS = 8
COLS = 16
B = 256
SLOTS = 3
EMB = 40
FEAT = 32
ALL = 2 * EMB + FEAT
PART = FEAT + 8


def halves(x):
    hi = x.astype(bf16).astype(f32)
    return hi, x - hi


def transposed_dot(a, b):
    return lax.dot_general(
        a, b, (((0,), (0,)), ((), ())), precision=HIGHEST, preferred_element_type=f32
    )


def kernel(
    emb_first, emb_second, signal, theta_first, theta_second, neighbors, w_forward, w_backward,
    out,
    emb1, emb2, theta1, theta2, near, wf, wb,
    home, rows, cols, right, left, xs, st, hot, idx, weight, acc,
    f_part, f_got, b_part, b_got, f_home, b_home, colx, rowx, f_part2, f_got2, b_part2, b_got2,
    in_sem, c_send, c_recv, r_send, r_recv, f_send, f_recv, b_send, b_recv,
    c2_send, c2_recv, r2_send, r2_recv, f2_send, f2_recv, b2_send, b2_recv,
):
    r = lax.axis_index("row")
    c = lax.axis_index("col")
    half = c // ROWS
    q = c % ROWS
    base = c - q
    user = base + r
    block_start = (2 * q + half) * (ROWS * B)
    same = q == r
    others = jnp.where(same, 0, 1).astype(i32)

    barrier = pltpu.get_barrier_semaphore()

    def greet(i, carry):
        pl.semaphore_signal(barrier, inc=1, device_id=(r, (c + i) % COLS), device_id_type=MESH)
        return carry

    def greet_columns(i, carry):
        k = (r + i) % ROWS

        @pl.when(jnp.logical_not(jnp.logical_and(same, k == r)))
        def _():
            pl.semaphore_signal(barrier, inc=1, device_id=(k, user), device_id_type=MESH)
            pl.semaphore_signal(barrier, inc=1, device_id=(q, base + k), device_id_type=MESH)

        return carry

    lax.fori_loop(1, COLS, greet, 0)
    lax.fori_loop(0, ROWS, greet_columns, 0)

    fetches = [
        pltpu.make_async_copy(src, dst, in_sem.at[n])
        for n, (src, dst) in enumerate(
            [
                (emb_first, emb1), (emb_second, emb2), (theta_first, theta1),
                (theta_second, theta2), (signal, home.at[pl.ds(2 * EMB, FEAT)]),
                (neighbors, near), (w_forward, wf), (w_backward, wb),
            ]
        )
    ]
    for fetch in fetches:
        fetch.start()
    for fetch in fetches[:5]:
        fetch.wait()
    home[0:EMB, :] = jnp.tanh(3.0 * transposed_dot(theta1[...], emb1[...]))
    home[EMB : 2 * EMB, :] = jnp.tanh(3.0 * transposed_dot(theta2[...], emb2[...]))

    pl.semaphore_wait(barrier, COLS - 1 + 2 * (ROWS - 1) + 2 * others)

    def to_users(k, src, dst, send, recv):
        return pltpu.make_async_remote_copy(
            src_ref=src, dst_ref=dst.at[q], send_sem=send.at[k], recv_sem=recv.at[q],
            device_id=(k, user), device_id_type=MESH,
        )

    def to_row(k, src, dst, send, recv):
        return pltpu.make_async_remote_copy(
            src_ref=src, dst_ref=dst.at[c], send_sem=send.at[k], recv_sem=recv.at[c],
            device_id=(r, k), device_id_type=MESH,
        )

    def to_homes(k, src, dst, send, recv):
        return pltpu.make_async_remote_copy(
            src_ref=src, dst_ref=dst.at[r], send_sem=send.at[k], recv_sem=recv.at[r],
            device_id=(q, base + k), device_id_type=MESH,
        )

    def arrival(dst, slot, send, recv):
        return pltpu.make_async_remote_copy(
            src_ref=dst.at[slot], dst_ref=dst.at[slot], send_sem=send.at[slot],
            recv_sem=recv.at[slot], device_id=(r, (c + 1) % COLS), device_id_type=MESH,
        )

    def share_with_users(src, dst, send, recv):
        def step(i, carry):
            k = (r + i) % ROWS

            @pl.when(jnp.logical_not(jnp.logical_and(same, k == r)))
            def _():
                to_users(k, src, dst, send, recv).start()

            return carry

        lax.fori_loop(0, ROWS, step, 0)

        @pl.when(same)
        def _():
            dst[q] = src[...]

    def from_homes(dst, send, recv):
        def step(k, carry):
            @pl.when(jnp.logical_not(jnp.logical_and(same, k == q)))
            def _():
                arrival(dst, k, send, recv).wait_recv()

            return carry

        lax.fori_loop(0, ROWS, step, 0)

    def share_with_row(src, dst, send, recv):
        def step(i, carry):
            to_row((c + COLS - i) % COLS, src, dst, send, recv).start()
            return carry

        lax.fori_loop(1, COLS, step, 0)
        dst[c] = src[...]

    share_with_users(home, cols, c_send, c_recv)
    share_with_row(home, rows, r_send, r_recv)

    fetches[5].wait()

    def find(g, carry):
        span = pl.ds(pl.multiple_of(g * B, B), B)
        local = near[:, span] - block_start
        slot = [jnp.full((1, B), -1, i32) for _ in range(SLOTS)]
        for k in range(near.shape[0]):
            entry = local[k : k + 1]
            inside = jnp.logical_and(entry >= 0, entry < ROWS * B)
            slot = [
                jnp.where(inside, entry, slot[0]),
                jnp.where(inside, slot[0], slot[1]),
                jnp.where(inside, slot[1], slot[2]),
            ]
        place = lax.broadcasted_iota(i32, (B, B), 0)
        for j in range(SLOTS):
            hot[g, :, j * B : (j + 1) * B] = (place == (slot[j] & (B - 1))).astype(f32).astype(bf16)
        idx[g] = jnp.concatenate(slot + [jnp.full((8 - SLOTS, B), -1, i32)], axis=0)
        return carry

    lax.fori_loop(0, COLS, find, 0)

    def put_columns(values, v):
        hi, lo = halves(values)
        xs[v * 64 : v * 64 + 64, :] = jnp.concatenate([hi, lo], axis=0).astype(bf16)

    from_homes(cols, c_send, c_recv)
    for v in range(ROWS):
        turned = jnp.concatenate([cols[v, EMB : 2 * EMB, :], -cols[v, 0:EMB, :]], axis=0)
        hi, lo = halves(turned)
        right[v * B : (v + 1) * B, :] = jnp.concatenate([hi, hi, lo], axis=0).T.astype(bf16)
        put_columns(cols[v, 2 * EMB : ALL, :], v)

    def forward(g):
        picked = jnp.dot(xs[...], hot[g], preferred_element_type=f32)
        total = jnp.zeros((FEAT, B), f32)
        for j in range(SLOTS):
            window = idx[g, j : j + 1, :] >> 8
            part = jnp.zeros((2 * FEAT, B), f32)
            for v in range(ROWS):
                part = jnp.where(
                    window == v, picked[v * 64 : v * 64 + 64, j * B : (j + 1) * B], part
                )
            total = total + weight[g, j : j + 1, :] * (part[:FEAT] + part[FEAT:])
        return total

    def first_step(i, carry):
        g = (c + i) % COLS

        @pl.when(i > 0)
        def _():
            arrival(rows, g, r_send, r_recv).wait_recv()

        hi, lo = halves(rows[g, 0 : 2 * EMB, :])
        left[...] = jnp.concatenate([hi, lo, hi], axis=0).astype(bf16)
        eight = lax.broadcasted_iota(i32, (8, B), 0)
        gap = [idx[g, j : j + 1, :] - eight for j in range(SLOTS)]
        found = [jnp.zeros((8, B), f32) for _ in range(SLOTS)]
        for v in range(ROWS):
            score = jnp.dot(
                right[v * B : (v + 1) * B, :], left[...], preferred_element_type=f32
            )
            for t in range(B // 8):
                for j in range(SLOTS):
                    found[j] = jnp.where(
                        gap[j] == v * B + 8 * t, score[8 * t : 8 * t + 8], found[j]
                    )
        sums = jnp.zeros((1, B), f32)
        for j in range(SLOTS):
            value = jnp.tanh(3.0 * jnp.sum(found[j], axis=0, keepdims=True))
            value = jnp.where(idx[g, j : j + 1, :] >= 0, jnp.maximum(value, 0.0), 0.0)
            weight[g, j : j + 1, :] = value
            sums = sums + value
        f_part[g, 0:FEAT, :] = forward(g)
        f_part[g, FEAT:PART, :] = jnp.broadcast_to(sums, (8, B))

        @pl.when(i > 0)
        def _():
            to_row(g, f_part.at[g], f_got, f_send, f_recv).start()

        return carry

    lax.fori_loop(0, COLS, first_step, 0)

    def backward(rows_of, ready, part, with_degree):
        acc[...] = jnp.zeros_like(acc)

        def step(i, carry):
            g = (c + i) % COLS
            ready(i, g)
            x = rows_of(g)
            for j in range(SLOTS):
                window = idx[g, j : j + 1, :] >> 8
                value = weight[g, j : j + 1, :]
                hi, lo = halves(x * value)
                both = jnp.concatenate([hi, lo], axis=0)
                for v in range(ROWS):
                    st[v * 64 : v * 64 + 64, j * B : (j + 1) * B] = jnp.where(
                        window == v, both, 0.0
                    ).astype(bf16)
                if with_degree:
                    hi, lo = halves(value)
                    mine = lax.broadcasted_iota(i32, (8, B), 0) == window
                    st[512:528, j * B : (j + 1) * B] = jnp.concatenate(
                        [jnp.where(mine, hi, 0.0), jnp.where(mine, lo, 0.0)], axis=0
                    ).astype(bf16)
            depth = 528 if with_degree else 512
            acc[0:depth, :] += lax.dot_general(
                st[0:depth, :], hot[g], (((1,), (1,)), ((), ())), preferred_element_type=f32
            )
            return carry

        lax.fori_loop(0, COLS, step, 0)
        for v in range(ROWS):
            part[v, 0:FEAT, :] = acc[v * 64 : v * 64 + 32, :] + acc[v * 64 + 32 : v * 64 + 64, :]
            if with_degree:
                part[v, FEAT:PART, :] = jnp.broadcast_to(
                    acc[512 + v : 513 + v, :] + acc[520 + v : 521 + v, :], (8, B)
                )

    def give_back(part, got, send, recv):
        def step(k, carry):
            @pl.when(jnp.logical_not(jnp.logical_and(same, k == q)))
            def _():
                to_homes(k, part.at[k], got, send, recv).start()

            return carry

        lax.fori_loop(0, ROWS, step, 0)

        @pl.when(same)
        def _():
            got[r] = part[q]

    def add_forward(part, got, send, recv):
        def step(i, total):
            k = (c + COLS - i) % COLS
            arrival(got, k, send, recv).wait_recv()
            return total + got[k]

        return lax.fori_loop(1, COLS, step, part[c])

    def add_backward(got, send, recv):
        def step(k, total):
            @pl.when(jnp.logical_not(jnp.logical_and(same, k == r)))
            def _():
                arrival(got, k, send, recv).wait_recv()

            return total + got[k]

        return lax.fori_loop(0, ROWS, step, jnp.zeros(got.shape[1:], f32))

    backward(lambda g: rows[g, 2 * EMB : ALL, :], lambda i, g: None, b_part, True)
    give_back(b_part, b_got, b_send, b_recv)

    own = home[2 * EMB : ALL, :]
    summed = add_forward(f_part, f_got, f_send, f_recv)
    f_scale = GO / (1.0 + summed[FEAT : FEAT + 1])
    f_home[...] = KEEP * own + (summed[:FEAT] + own) * f_scale
    share_with_users(f_home, colx, c2_send, c2_recv)

    summed = add_backward(b_got, b_send, b_recv)
    b_scale = GO / (1.0 + summed[FEAT : FEAT + 1])
    b_home[...] = KEEP * own + (summed[:FEAT] + own) * b_scale
    share_with_row(b_home, rowx, r2_send, r2_recv)

    from_homes(colx, c2_send, c2_recv)
    for v in range(ROWS):
        put_columns(colx[v], v)

    def second_step(i, carry):
        g = (c + i) % COLS
        f_part2[g] = forward(g)

        @pl.when(i > 0)
        def _():
            to_row(g, f_part2.at[g], f_got2, f2_send, f2_recv).start()

        return carry

    lax.fori_loop(0, COLS, second_step, 0)

    def ready(i, g):
        @pl.when(i > 0)
        def _():
            arrival(rowx, g, r2_send, r2_recv).wait_recv()

    backward(lambda g: rowx[g], ready, b_part2, False)
    give_back(b_part2, b_got2, b2_send, b2_recv)

    fetches[6].wait()
    fetches[7].wait()
    first = f_home[...]
    summed = add_forward(f_part2, f_got2, f2_send, f2_recv)
    second = KEEP * own + (summed + first) * f_scale
    mixed = transposed_dot(wf[...], jnp.concatenate([own, first, second], axis=0))
    first = b_home[...]
    summed = add_backward(b_got2, b2_send, b2_recv)
    second = KEEP * own + (summed + first) * b_scale
    out[...] = mixed + transposed_dot(wb[...], jnp.concatenate([own, first, second], axis=0))

    def sent_to_users(k, carry):
        @pl.when(jnp.logical_not(jnp.logical_and(same, k == r)))
        def _():
            to_users(k, home, cols, c_send, c_recv).wait_send()
            to_users(k, f_home, colx, c2_send, c2_recv).wait_send()

        @pl.when(jnp.logical_not(jnp.logical_and(same, k == q)))
        def _():
            to_homes(k, b_part.at[k], b_got, b_send, b_recv).wait_send()
            to_homes(k, b_part2.at[k], b_got2, b2_send, b2_recv).wait_send()

        return carry

    def sent_to_row(i, carry):
        k = (c + i) % COLS
        to_row(k, home, rows, r_send, r_recv).wait_send()
        to_row(k, f_part.at[k], f_got, f_send, f_recv).wait_send()
        to_row(k, b_home, rowx, r2_send, r2_recv).wait_send()
        to_row(k, f_part2.at[k], f_got2, f2_send, f2_recv).wait_send()
        return carry

    lax.fori_loop(0, ROWS, sent_to_users, 0)
    lax.fori_loop(1, COLS, sent_to_row, 0)


def per_device(*args):
    vmem = pltpu.VMEM
    keep_count = args[5].shape[0]
    dma = pltpu.SemaphoreType.DMA
    scratch = [
        vmem((EMB, B), f32), vmem((EMB, B), f32), vmem((EMB, EMB), f32), vmem((EMB, EMB), f32),
        vmem((keep_count, COLS * B), i32), vmem((3 * FEAT, FEAT), f32), vmem((3 * FEAT, FEAT), f32),
        vmem((ALL, B), f32),
        vmem((COLS, ALL, B), f32),
        vmem((ROWS, ALL, B), f32),
        vmem((ROWS * B, 6 * EMB), bf16),
        vmem((6 * EMB, B), bf16),
        vmem((512, B), bf16),
        vmem((528, SLOTS * B), bf16),
        vmem((COLS, B, SLOTS * B), bf16),
        vmem((COLS, 8, B), i32),
        vmem((COLS, 8, B), f32),
        vmem((528, B), f32),
        vmem((COLS, PART, B), f32), vmem((COLS, PART, B), f32),
        vmem((ROWS, PART, B), f32), vmem((ROWS, PART, B), f32),
        vmem((FEAT, B), f32), vmem((FEAT, B), f32),
        vmem((ROWS, FEAT, B), f32), vmem((COLS, FEAT, B), f32),
        vmem((COLS, FEAT, B), f32), vmem((COLS, FEAT, B), f32),
        vmem((ROWS, FEAT, B), f32), vmem((ROWS, FEAT, B), f32),
        dma((8,)),
    ]
    for count in (ROWS, COLS, COLS, ROWS, ROWS, COLS, COLS, ROWS):
        scratch += [dma((count,)), dma((count,))]
    return pl.pallas_call(
        kernel,
        out_shape=jax.ShapeDtypeStruct((FEAT, B), f32),
        in_specs=[pl.BlockSpec(memory_space=pl.ANY)] * 8,
        out_specs=pl.BlockSpec(memory_space=pltpu.VMEM),
        scratch_shapes=scratch,
        compiler_params=pltpu.CompilerParams(
            collective_id=0, has_side_effects=True, vmem_limit_bytes=48 * 1024 * 1024
        ),
        name="graph_layer",
    )(*args)


def solution(mesh):
    placed = (
        P(None, ("row", "col")),
        P(None, ("row", "col")),
        P(None, ("row", "col")),
        P(),
        P(),
        P(None, "row"),
        P(),
        P(),
    )
    return jax.shard_map(
        per_device, mesh=mesh, in_specs=placed, out_specs=P(None, ("row", "col")), check_vma=False
    )
```

time: 1150 us -> 137 us (0.12)
  the two profiles are of different devices: /device:TPU:1 before, /device:TPU:29 now
where the time goes in v1:
time: 137 us
  Pallas kernels  132 us (96%)
  local copies, waits for them, and re-layouts  4.7 us (3%)
    pallas_call x1, Pallas kernels, per_device(): pl.pallas_call(kernel, out_shape=jax.ShapeDtypeStruct((FEAT, B), f32), in...  132 us
    unnamed x15, local copies, waits for them, and re-layouts  4.7 us

profile of v1, /device:TPU:29, one launch (start us, length us, event | category | flops | bytes accessed | tf_op | source)
XLA Modules:
  0.0 136.9 jit_solution(14745094156679343815)
XLA Ops:
  0.0 0.0 copy-start.2
  0.0 0.0 copy-start.3
  0.0 0.8 copy.9.w_forward
  0.8 0.0 copy-start.1
  0.8 0.8 copy.10.w_backward
  1.6 0.0 copy-done.2
  1.7 0.0 copy-done.3
  1.7 0.0 copy-done.1
  1.7 0.0 copy-start
  1.7 1.0 copy-done
  2.7 0.0 copy-start.4
  2.7 0.7 copy-done.4
  3.4 0.0 copy-start.5
  3.4 0.7 copy-done.5
  4.1 132.2 %graph_layer.1 = f32[32,256]{1,0:T(8,128)S(1)} custom-call(f32[40,256]{1,0:T(8,128)S(1)} %copy-done.1, f32[40,256]{1,0:T(8,128)S(1)} %copy-done.2, f32[32,256]{1,0:T(8,128)S(1)} %copy-done.3, f32[40,40]{1,0:T(8,128)S(1)} %copy-done.4, f32[40,40]{1,0:T(8,128)S(1)} %copy-done.5, s32[20,4096]{1,0:T(8,128)S(1)} %copy-done, f32[96,32]{1,0:T(8,128)S(1)} %copy.9.w_forward, ...), custom_call_target="tpu_custom_call" | custom-call | tf_op jit(solution)/shard_map/graph_layer/pallas_call | solution.py:407
  136.3 0.6 copy.12
Async XLA Ops:
  0.0 1.6 %copy-start.2 = (f32[40,256]{1,0:T(8,128)S(1)}, f32[40,256]{1,0:T(8,128)}, u32[]{:S(2)}) copy-start(f32[40,256]{1,0:T(8,128)} %emb_second.1) | copy-start | bytes 122884
  0.0 1.7 %copy-start.3 = (f32[32,256]{1,0:T(8,128)S(1)}, f32[32,256]{1,0:T(8,128)}, u32[]{:S(2)}) copy-start(f32[32,256]{1,0:T(8,128)} %signal.1) | copy-start | bytes 98308
  0.8 0.8 copy-start.1
  1.7 1.0 copy-start
  2.7 0.7 copy-start.4
  3.4 0.7 copy-start.5

commit v2 on v1

--- a/solution.py
+++ b/solution.py
@@ -18,6 +18,8 @@
 EMB = 40
 FEAT = 32
 ALL = 2 * EMB + FEAT
+HALF1 = 8
+HALF2 = 8
 PART = FEAT + 8
 
 
@@ -36,19 +38,26 @@
     emb_first, emb_second, signal, theta_first, theta_second, neighbors, w_forward, w_backward,
     out,
     emb1, emb2, theta1, theta2, near, wf, wb,
-    home, rows, cols, right, left, xs, st, hot, idx, weight, acc,
-    f_part, f_got, b_part, b_got, f_home, b_home, colx, rowx, f_part2, f_got2, b_part2, b_got2,
-    in_sem, c_send, c_recv, r_send, r_recv, f_send, f_recv, b_send, b_recv,
-    c2_send, c2_recv, r2_send, r2_recv, f2_send, f2_recv, b2_send, b2_recv,
+    rows, cols, right, left, xs, st, hot, idx, weight, acc,
+    f_part, f_got, b_part, b_got, f_home, colx, rowx, f_part2, f_got2, b_part2, b_got2,
+    in_sem, cm_send, cm_recv, cs_send, cs_recv, rm_send, rm_recv, rs_send, rs_recv,
+    f_send, f_recv, b_send, b_recv, c2_send, c2_recv, r2_send, r2_recv,
+    f2_send, f2_recv, b2_send, b2_recv,
 ):
     r = lax.axis_index("row")
     c = lax.axis_index("col")
     half = c // ROWS
     q = c % ROWS
     base = c - q
-    user = base + r
-    block_start = (2 * q + half) * (ROWS * B)
-    same = q == r
+    z, x_lo = r // 2, r % 2
+    maker = (z + 2 * (c % 2) + (c // 2) % 2) % 4 * 2 + (x_lo + (c // 4) % 2) % 2
+    block_start = (2 * maker + half) * (ROWS * B)
+    same = q == 0
+
+    def user(k):
+        away = (z + 4 - k // 2) % 4
+        return base + 4 * ((x_lo + k) % 2) + 2 * (away % 2) + away // 2
+
     others = jnp.where(same, 0, 1).astype(i32)
 
     barrier = pltpu.get_barrier_semaphore()
@@ -57,13 +66,14 @@
         pl.semaphore_signal(barrier, inc=1, device_id=(r, (c + i) % COLS), device_id_type=MESH)
         return carry
 
-    def greet_columns(i, carry):
-        k = (r + i) % ROWS
-
+    def greet_columns(k, carry):
         @pl.when(jnp.logical_not(jnp.logical_and(same, k == r)))
         def _():
-            pl.semaphore_signal(barrier, inc=1, device_id=(k, user), device_id_type=MESH)
-            pl.semaphore_signal(barrier, inc=1, device_id=(q, base + k), device_id_type=MESH)
+            pl.semaphore_signal(barrier, inc=1, device_id=(k, user(k)), device_id_type=MESH)
+
+        @pl.when(jnp.logical_not(jnp.logical_and(same, k == q)))
+        def _():
+            pl.semaphore_signal(barrier, inc=1, device_id=(maker, base + k), device_id_type=MESH)
 
         return carry
 
@@ -75,7 +85,7 @@
         for n, (src, dst) in enumerate(
             [
                 (emb_first, emb1), (emb_second, emb2), (theta_first, theta1),
-                (theta_second, theta2), (signal, home.at[pl.ds(2 * EMB, FEAT)]),
+                (theta_second, theta2), (signal, rows.at[c, pl.ds(2 * EMB, FEAT)]),
                 (neighbors, near), (w_forward, wf), (w_backward, wb),
             ]
         )
@@ -84,15 +94,15 @@
         fetch.start()
     for fetch in fetches[:5]:
         fetch.wait()
-    home[0:EMB, :] = jnp.tanh(3.0 * transposed_dot(theta1[...], emb1[...]))
-    home[EMB : 2 * EMB, :] = jnp.tanh(3.0 * transposed_dot(theta2[...], emb2[...]))
+    rows[c, 0:EMB, :] = jnp.tanh(3.0 * transposed_dot(theta1[...], emb1[...]))
+    rows[c, EMB : 2 * EMB, :] = jnp.tanh(3.0 * transposed_dot(theta2[...], emb2[...]))
 
     pl.semaphore_wait(barrier, COLS - 1 + 2 * (ROWS - 1) + 2 * others)
 
     def to_users(k, src, dst, send, recv):
         return pltpu.make_async_remote_copy(
             src_ref=src, dst_ref=dst.at[q], send_sem=send.at[k], recv_sem=recv.at[q],
-            device_id=(k, user), device_id_type=MESH,
+            device_id=(k, user(k)), device_id_type=MESH,
         )
 
     def to_row(k, src, dst, send, recv):
@@ -104,7 +114,7 @@
     def to_homes(k, src, dst, send, recv):
         return pltpu.make_async_remote_copy(
             src_ref=src, dst_ref=dst.at[r], send_sem=send.at[k], recv_sem=recv.at[r],
-            device_id=(q, base + k), device_id_type=MESH,
+            device_id=(maker, base + k), device_id_type=MESH,
         )
 
     def arrival(dst, slot, send, recv):
@@ -113,42 +123,102 @@
             recv_sem=recv.at[slot], device_id=(r, (c + 1) % COLS), device_id_type=MESH,
         )
 
-    def share_with_users(src, dst, send, recv):
+    def twin(k):
+        return k + 1 - 2 * (k % 2)
+
+    def across(k):
+        return k + 2 - 4 * ((k // 2) % 2)
+
+    def around(k, n):
+        return (k + 4 * n) % COLS
+
+    def order(t):
+        i = t // 2
+        k = i // 2
+        slot = around(c, k + (k // 2) * (1 - 2 * (k % 2)))
+        slot = slot + (i % 2) * (2 - 4 * ((slot // 2) % 2))
+        return slot + (t % 2) * (1 - 2 * (slot % 2))
+
+    M = pl.ds(0, 2 * EMB)
+    S = pl.ds(2 * EMB, FEAT)
+
+    def pass_on(to, src_buf, slot, dst_buf, part, n, send, recv):
+        return pltpu.make_async_remote_copy(
+            src_ref=src_buf.at[slot, part], dst_ref=dst_buf.at[slot, part],
+            send_sem=send.at[n], recv_sem=recv.at[slot],
+            device_id=(r, to), device_id_type=MESH,
+        )
+
+    def row_arrival(buf, slot, part, send, recv):
+        return pltpu.make_async_remote_copy(
+            src_ref=buf.at[slot, part], dst_ref=buf.at[slot, part], send_sem=send.at[0],
+            recv_sem=recv.at[slot], device_id=(r, twin(c)), device_id_type=MESH,
+        )
+
+    def users_each(do):
         def step(i, carry):
             k = (r + i) % ROWS
 
             @pl.when(jnp.logical_not(jnp.logical_and(same, k == r)))
             def _():
-                to_users(k, src, dst, send, recv).start()
+                do(k)
 
             return carry
 
         lax.fori_loop(0, ROWS, step, 0)
 
-        @pl.when(same)
-        def _():
-            dst[q] = src[...]
-
-    def from_homes(dst, send, recv):
+    def home_to(k, part, send, recv):
+        return pltpu.make_async_remote_copy(
+            src_ref=rows.at[c, part], dst_ref=cols.at[q, part], send_sem=send.at[k],
+            recv_sem=recv.at[q], device_id=(k, user(k)), device_id_type=MESH,
+        )
+
+    def homes_arrived(buf, part, send, recv):
         def step(k, carry):
             @pl.when(jnp.logical_not(jnp.logical_and(same, k == q)))
             def _():
-                arrival(dst, k, send, recv).wait_recv()
+                pltpu.make_async_remote_copy(
+                    src_ref=buf.at[k, part], dst_ref=buf.at[k, part], send_sem=send.at[k],
+                    recv_sem=recv.at[k], device_id=(r, twin(c)), device_id_type=MESH,
+                ).wait_recv()
 
             return carry
 
         lax.fori_loop(0, ROWS, step, 0)
 
-    def share_with_row(src, dst, send, recv):
-        def step(i, carry):
-            to_row((c + COLS - i) % COLS, src, dst, send, recv).start()
-            return carry
-
-        lax.fori_loop(1, COLS, step, 0)
-        dst[c] = src[...]
-
-    share_with_users(home, cols, c_send, c_recv)
-    share_with_row(home, rows, r_send, r_recv)
+    def share_with_users(src, dst, send, recv):
+        users_each(lambda k: to_users(k, src, dst, send, recv).start())
+
+        @pl.when(same)
+        def _():
+            dst[q] = src[...]
+
+    def row_copies(buf, part, send, recv):
+        far = [around(c, 1), around(c, 3), around(c, 2)]
+        make = lambda to, slot, n: pass_on(to, buf, slot, buf, part, n, send, recv)
+        mine = [make(across(c), c, 0)] + [make(to, c, 1 + n) for n, to in enumerate(far)]
+        mine += [make(twin(c), c, 4)]
+        relayed = [make(to, across(c), 5 + n) for n, to in enumerate(far)]
+        relayed += [make(twin(c), across(c), 8)]
+        return mine, relayed
+
+    def to_twin(i, buf, part, send, recv):
+        return pass_on(twin(c), buf, order(2 * i), buf, part, 7 + i, send, recv)
+
+    m_mine, m_relayed = row_copies(rows, M, rm_send, rm_recv)
+    s_mine, s_relayed = row_copies(rows, S, rs_send, rs_recv)
+    m_mine[0].start()
+    users_each(lambda k: home_to(k, M, cm_send, cm_recv).start())
+    for copy in m_mine[1:]:
+        copy.start()
+    s_mine[0].start()
+    users_each(lambda k: home_to(k, S, cs_send, cs_recv).start())
+    for copy in s_mine[1:]:
+        copy.start()
+
+    @pl.when(same)
+    def _():
+        cols[q] = rows[c]
 
     fetches[5].wait()
 
@@ -176,12 +246,14 @@
         hi, lo = halves(values)
         xs[v * 64 : v * 64 + 64, :] = jnp.concatenate([hi, lo], axis=0).astype(bf16)
 
-    from_homes(cols, c_send, c_recv)
+    row_arrival(rows, across(c), M, rm_send, rm_recv).wait_recv()
+    for copy in m_relayed:
+        copy.start()
+    homes_arrived(cols, M, cm_send, cm_recv)
     for v in range(ROWS):
         turned = jnp.concatenate([cols[v, EMB : 2 * EMB, :], -cols[v, 0:EMB, :]], axis=0)
         hi, lo = halves(turned)
         right[v * B : (v + 1) * B, :] = jnp.concatenate([hi, hi, lo], axis=0).T.astype(bf16)
-        put_columns(cols[v, 2 * EMB : ALL, :], v)
 
     def forward(g):
         picked = jnp.dot(xs[...], hot[g], preferred_element_type=f32)
@@ -196,12 +268,22 @@
             total = total + weight[g, j : j + 1, :] * (part[:FEAT] + part[FEAT:])
         return total
 
-    def first_step(i, carry):
-        g = (c + i) % COLS
-
-        @pl.when(i > 0)
-        def _():
-            arrival(rows, g, r_send, r_recv).wait_recv()
+    def score_step(t, carry):
+        g = order(t)
+
+        @pl.when(jnp.logical_or(t % 2 == 1, t >= 4))
+        def _():
+            row_arrival(rows, g, M, rm_send, rm_recv).wait_recv()
+
+        @pl.when(jnp.logical_and(t % 2 == 0, t >= 4))
+        def _():
+            to_twin(t // 2, rows, M, rm_send, rm_recv).start()
+
+        @pl.when(t == 4)
+        def _():
+            row_arrival(rows, across(c), S, rs_send, rs_recv).wait_recv()
+            for copy in s_relayed:
+                copy.start()
 
         hi, lo = halves(rows[g, 0 : 2 * EMB, :])
         left[...] = jnp.concatenate([hi, lo, hi], axis=0).astype(bf16)
@@ -223,10 +305,25 @@
             value = jnp.where(idx[g, j : j + 1, :] >= 0, jnp.maximum(value, 0.0), 0.0)
             weight[g, j : j + 1, :] = value
             sums = sums + value
+        f_part[g, FEAT:PART, :] = jnp.broadcast_to(sums, (8, B))
+        return carry
+
+    lax.fori_loop(0, COLS, score_step, 0)
+    homes_arrived(cols, S, cs_send, cs_recv)
+    for v in range(ROWS):
+        put_columns(cols[v, 2 * EMB : ALL, :], v)
+
+    def first_step(t, carry):
+        g = order((t + 1) % COLS)
+
+        @pl.when(jnp.logical_and(t % 2 == 0, t >= 4))
+        def _():
+            row_arrival(rows, order(t), S, rs_send, rs_recv).wait_recv()
+            to_twin(t // 2, rows, S, rs_send, rs_recv).start()
+
         f_part[g, 0:FEAT, :] = forward(g)
-        f_part[g, FEAT:PART, :] = jnp.broadcast_to(sums, (8, B))
-
-        @pl.when(i > 0)
+
+        @pl.when(t < COLS - 1)
         def _():
             to_row(g, f_part.at[g], f_got, f_send, f_recv).start()
 
@@ -234,12 +331,13 @@
 
     lax.fori_loop(0, COLS, first_step, 0)
 
-    def backward(rows_of, ready, part, with_degree):
-        acc[...] = jnp.zeros_like(acc)
-
-        def step(i, carry):
-            g = (c + i) % COLS
-            ready(i, g)
+    def backward(first, last, rows_of, ready, with_degree):
+        if first == 0:
+            acc[...] = jnp.zeros_like(acc)
+
+        def step(t, carry):
+            g = order(t)
+            ready(t, g)
             x = rows_of(g)
             for j in range(SLOTS):
                 window = idx[g, j : j + 1, :] >> 8
@@ -262,7 +360,9 @@
             )
             return carry
 
-        lax.fori_loop(0, COLS, step, 0)
+        lax.fori_loop(first, last, step, 0)
+
+    def keep_backward(part, with_degree):
         for v in range(ROWS):
             part[v, 0:FEAT, :] = acc[v * 64 : v * 64 + 32, :] + acc[v * 64 + 32 : v * 64 + 64, :]
             if with_degree:
@@ -302,42 +402,69 @@
 
         return lax.fori_loop(0, ROWS, step, jnp.zeros(got.shape[1:], f32))
 
-    backward(lambda g: rows[g, 2 * EMB : ALL, :], lambda i, g: None, b_part, True)
-    give_back(b_part, b_got, b_send, b_recv)
-
-    own = home[2 * EMB : ALL, :]
+    def signal_ready(t, g):
+        @pl.when(t % 2 == 1)
+        def _():
+            row_arrival(rows, g, S, rs_send, rs_recv).wait_recv()
+
+    own_signal = lambda g: rows[g, 2 * EMB : ALL, :]
+    backward(0, HALF1, own_signal, signal_ready, True)
+
+    own = rows[c, 2 * EMB : ALL, :]
     summed = add_forward(f_part, f_got, f_send, f_recv)
     f_scale = GO / (1.0 + summed[FEAT : FEAT + 1])
     f_home[...] = KEEP * own + (summed[:FEAT] + own) * f_scale
     share_with_users(f_home, colx, c2_send, c2_recv)
 
+    backward(HALF1, COLS, own_signal, signal_ready, True)
+    keep_backward(b_part, True)
+    give_back(b_part, b_got, b_send, b_recv)
+
+    homes_arrived(colx, pl.ds(0, FEAT), c2_send, c2_recv)
+    for v in range(ROWS):
+        put_columns(colx[v], v)
+
+    def second_step(t, carry):
+        g = order(t + 1)
+        f_part2[g] = forward(g)
+        to_row(g, f_part2.at[g], f_got2, f2_send, f2_recv).start()
+        return carry
+
+    lax.fori_loop(0, HALF2, second_step, 0)
+
     summed = add_backward(b_got, b_send, b_recv)
     b_scale = GO / (1.0 + summed[FEAT : FEAT + 1])
-    b_home[...] = KEEP * own + (summed[:FEAT] + own) * b_scale
-    share_with_row(b_home, rowx, r2_send, r2_recv)
-
-    from_homes(colx, c2_send, c2_recv)
-    for v in range(ROWS):
-        put_columns(colx[v], v)
-
-    def second_step(i, carry):
-        g = (c + i) % COLS
-        f_part2[g] = forward(g)
-
-        @pl.when(i > 0)
-        def _():
-            to_row(g, f_part2.at[g], f_got2, f2_send, f2_recv).start()
-
-        return carry
-
-    lax.fori_loop(0, COLS, second_step, 0)
-
-    def ready(i, g):
-        @pl.when(i > 0)
-        def _():
-            arrival(rowx, g, r2_send, r2_recv).wait_recv()
-
-    backward(lambda g: rowx[g], ready, b_part2, False)
+    rowx[c] = KEEP * own + (summed[:FEAT] + own) * b_scale
+    A = pl.ds(0, FEAT)
+    x_mine, x_relayed = row_copies(rowx, A, r2_send, r2_recv)
+    for copy in x_mine:
+        copy.start()
+
+    def relay(t):
+        @pl.when(t == HALF2 + 2)
+        def _():
+            row_arrival(rowx, across(c), A, r2_send, r2_recv).wait_recv()
+            for copy in x_relayed:
+                copy.start()
+
+    def second_late(t, carry):
+        relay(t)
+        return second_step(t, carry)
+
+    lax.fori_loop(HALF2, COLS - 1, second_late, 0)
+    f_part2[c] = forward(c)
+
+    def ready(t, g):
+        @pl.when(jnp.logical_or(t % 2 == 1, t >= 4))
+        def _():
+            row_arrival(rowx, g, A, r2_send, r2_recv).wait_recv()
+
+        @pl.when(jnp.logical_and(t % 2 == 0, t >= 4))
+        def _():
+            to_twin(t // 2, rowx, A, r2_send, r2_recv).start()
+
+    backward(0, COLS, lambda g: rowx[g], ready, False)
+    keep_backward(b_part2, False)
     give_back(b_part2, b_got2, b2_send, b2_recv)
 
     fetches[6].wait()
@@ -346,17 +473,19 @@
     summed = add_forward(f_part2, f_got2, f2_send, f2_recv)
     second = KEEP * own + (summed + first) * f_scale
     mixed = transposed_dot(wf[...], jnp.concatenate([own, first, second], axis=0))
-    first = b_home[...]
+    first = rowx[c]
     summed = add_backward(b_got2, b2_send, b2_recv)
     second = KEEP * own + (summed + first) * b_scale
     out[...] = mixed + transposed_dot(wb[...], jnp.concatenate([own, first, second], axis=0))
 
-    def sent_to_users(k, carry):
-        @pl.when(jnp.logical_not(jnp.logical_and(same, k == r)))
-        def _():
-            to_users(k, home, cols, c_send, c_recv).wait_send()
-            to_users(k, f_home, colx, c2_send, c2_recv).wait_send()
-
+    def sent(k):
+        home_to(k, M, cm_send, cm_recv).wait_send()
+        home_to(k, S, cs_send, cs_recv).wait_send()
+        to_users(k, f_home, colx, c2_send, c2_recv).wait_send()
+
+    users_each(sent)
+
+    def sent_to_homes(k, carry):
         @pl.when(jnp.logical_not(jnp.logical_and(same, k == q)))
         def _():
             to_homes(k, b_part.at[k], b_got, b_send, b_recv).wait_send()
@@ -366,14 +495,22 @@
 
     def sent_to_row(i, carry):
         k = (c + i) % COLS
-        to_row(k, home, rows, r_send, r_recv).wait_send()
         to_row(k, f_part.at[k], f_got, f_send, f_recv).wait_send()
-        to_row(k, b_home, rowx, r2_send, r2_recv).wait_send()
         to_row(k, f_part2.at[k], f_got2, f2_send, f2_recv).wait_send()
         return carry
 
-    lax.fori_loop(0, ROWS, sent_to_users, 0)
+    lax.fori_loop(0, ROWS, sent_to_homes, 0)
     lax.fori_loop(1, COLS, sent_to_row, 0)
+    for copy in m_mine + m_relayed + s_mine + s_relayed + x_mine + x_relayed:
+        copy.wait_send()
+
+    def sent_to_twin(i, carry):
+        to_twin(i, rows, M, rm_send, rm_recv).wait_send()
+        to_twin(i, rows, S, rs_send, rs_recv).wait_send()
+        to_twin(i, rowx, A, r2_send, r2_recv).wait_send()
+        return carry
+
+    lax.fori_loop(2, ROWS, sent_to_twin, 0)
 
 
 def per_device(*args):
@@ -383,7 +520,6 @@
     scratch = [
         vmem((EMB, B), f32), vmem((EMB, B), f32), vmem((EMB, EMB), f32), vmem((EMB, EMB), f32),
         vmem((keep_count, COLS * B), i32), vmem((3 * FEAT, FEAT), f32), vmem((3 * FEAT, FEAT), f32),
-        vmem((ALL, B), f32),
         vmem((COLS, ALL, B), f32),
         vmem((ROWS, ALL, B), f32),
         vmem((ROWS * B, 6 * EMB), bf16),
@@ -396,13 +532,13 @@
         vmem((528, B), f32),
         vmem((COLS, PART, B), f32), vmem((COLS, PART, B), f32),
         vmem((ROWS, PART, B), f32), vmem((ROWS, PART, B), f32),
-        vmem((FEAT, B), f32), vmem((FEAT, B), f32),
+        vmem((FEAT, B), f32),
         vmem((ROWS, FEAT, B), f32), vmem((COLS, FEAT, B), f32),
         vmem((COLS, FEAT, B), f32), vmem((COLS, FEAT, B), f32),
         vmem((ROWS, FEAT, B), f32), vmem((ROWS, FEAT, B), f32),
         dma((8,)),
     ]
-    for count in (ROWS, COLS, COLS, ROWS, ROWS, COLS, COLS, ROWS):
+    for count in (ROWS, ROWS, COLS, COLS, COLS, ROWS, ROWS, COLS, COLS, ROWS):
         scratch += [dma((count,)), dma((count,))]
     return pl.pallas_call(
         kernel,

time: 137 us -> 93.7 us (0.68)
  the two profiles are of different devices: /device:TPU:29 before, /device:TPU:1 now
where the time goes in v2:
time: 93.7 us; the launch traced here: 92.9 us
  Pallas kernels  88.2 us (94%)
  local copies, waits for them, and re-layouts  4.7 us (5%)
    pallas_call x1, Pallas kernels, per_device(): pl.pallas_call(kernel, out_shape=jax.ShapeDtypeStruct((FEAT, B), f32), in...  88.2 us
    unnamed x15, local copies, waits for them, and re-layouts  4.7 us

profile of v2, /device:TPU:1, one launch (start us, length us, event | category | flops | bytes accessed | tf_op | source)
XLA Modules:
  0.0 92.9 jit_solution(5467072204908433714)
XLA Ops:
  0.0 0.0 copy-start.2
  0.0 0.0 copy-start.3
  0.0 0.8 copy.9.w_forward
  0.8 0.0 copy-start.1
  0.8 0.8 copy.10.w_backward
  1.6 0.0 copy-done.2
  1.7 0.0 copy-done.3
  1.7 0.0 copy-done.1
  1.7 0.0 copy-start
  1.7 1.0 %copy-done = s32[20,4096]{1,0:T(8,128)S(1)} copy-done((s32[20,4096]{1,0:T(8,128)S(1)}, s32[20,4096]{1,0:T(8,128)}, u32[]{:S(2)}) %copy-start) | copy-done | bytes 327704
  2.7 0.0 copy-start.4
  2.7 0.7 copy-done.4
  3.4 0.0 copy-start.5
  3.4 0.7 copy-done.5
  4.1 88.2 %graph_layer.1 = f32[32,256]{1,0:T(8,128)S(1)} custom-call(f32[40,256]{1,0:T(8,128)S(1)} %copy-done.1, f32[40,256]{1,0:T(8,128)S(1)} %copy-done.2, f32[32,256]{1,0:T(8,128)S(1)} %copy-done.3, f32[40,40]{1,0:T(8,128)S(1)} %copy-done.4, f32[40,40]{1,0:T(8,128)S(1)} %copy-done.5, s32[20,4096]{1,0:T(8,128)S(1)} %copy-done, f32[96,32]{1,0:T(8,128)S(1)} %copy.9.w_forward, ...), custom_call_target="tpu_custom_call" | custom-call | tf_op jit(solution)/shard_map/graph_layer/pallas_call | solution.py:543
  92.3 0.6 copy.12
Async XLA Ops:
  0.0 1.6 %copy-start.2 = (f32[40,256]{1,0:T(8,128)S(1)}, f32[40,256]{1,0:T(8,128)}, u32[]{:S(2)}) copy-start(f32[40,256]{1,0:T(8,128)} %emb_second.1) | copy-start | bytes 122884
  0.0 1.7 %copy-start.3 = (f32[32,256]{1,0:T(8,128)S(1)}, f32[32,256]{1,0:T(8,128)}, u32[]{:S(2)}) copy-start(f32[32,256]{1,0:T(8,128)} %signal.1) | copy-start | bytes 98308
  0.8 0.8 copy-start.1
  1.7 1.0 %copy-start = (s32[20,4096]{1,0:T(8,128)S(1)}, s32[20,4096]{1,0:T(8,128)}, u32[]{:S(2)}) copy-start(s32[20,4096]{1,0:T(8,128)} %neighbors.1) | copy-start | bytes 983044
  2.7 0.7 copy-start.4
  3.4 0.7 copy-start.5

commit v3 on v2

--- a/solution.py
+++ b/solution.py
@@ -18,8 +18,9 @@
 EMB = 40
 FEAT = 32
 ALL = 2 * EMB + FEAT
-HALF1 = 8
-HALF2 = 8
+VMEM_BYTES = 60 * 1024 * 1024
+SPREAD_AT = 8
+STEP = 4
 PART = FEAT + 8
 
 
@@ -34,15 +35,20 @@
     )
 
 
+def full_dot(a, b):
+    return jnp.dot(a, b, precision=HIGHEST, preferred_element_type=f32)
+
+
 def kernel(
     emb_first, emb_second, signal, theta_first, theta_second, neighbors, w_forward, w_backward,
     out,
     emb1, emb2, theta1, theta2, near, wf, wb,
-    rows, cols, right, left, xs, st, hot, idx, weight, acc,
-    f_part, f_got, b_part, b_got, f_home, colx, rowx, f_part2, f_got2, b_part2, b_got2,
-    in_sem, cm_send, cm_recv, cs_send, cs_recv, rm_send, rm_recv, rs_send, rs_recv,
+    rows, cols, levels, right, left, xs, st, hot, idx, weight, acc,
+    f_part, f_pair, f_got, b_part, b_got, f_home, colx, rowx, f_part2, f_pair2, f_got2, b_part2, b_got2,
+    in_sem, lm_send, lm_recv, ls_send, ls_recv, cm_send, cm_recv, cs_send, cs_recv,
+    rm_send, rm_recv, rs_send, rs_recv,
     f_send, f_recv, b_send, b_recv, c2_send, c2_recv, r2_send, r2_recv,
-    f2_send, f2_recv, b2_send, b2_recv,
+    f2_send, f2_recv, b2_send, b2_recv, p_send, p_recv, p2_send, p2_recv,
 ):
     r = lax.axis_index("row")
     c = lax.axis_index("col")
@@ -78,6 +84,18 @@
         return carry
 
     lax.fori_loop(1, COLS, greet, 0)
+    for n in range(1, 4):
+        pl.semaphore_signal(
+            barrier, inc=1, device_id=((z + n) % 4 * 2 + x_lo, c), device_id_type=MESH
+        )
+
+    @pl.when((c // 4) % 2 == 1)
+    def _():
+        for n in range(4):
+            pl.semaphore_signal(
+                barrier, inc=1, device_id=(2 * z + 1 - x_lo, c - c % 4 + n), device_id_type=MESH
+            )
+
     lax.fori_loop(0, ROWS, greet_columns, 0)
 
     fetches = [
@@ -97,7 +115,7 @@
     rows[c, 0:EMB, :] = jnp.tanh(3.0 * transposed_dot(theta1[...], emb1[...]))
     rows[c, EMB : 2 * EMB, :] = jnp.tanh(3.0 * transposed_dot(theta2[...], emb2[...]))
 
-    pl.semaphore_wait(barrier, COLS - 1 + 2 * (ROWS - 1) + 2 * others)
+    pl.semaphore_wait(barrier, COLS - 1 + 2 * (ROWS - 1) + 2 * others + 3 + 4 * ((c // 4) % 2))
 
     def to_users(k, src, dst, send, recv):
         return pltpu.make_async_remote_copy(
@@ -167,15 +185,64 @@
 
         lax.fori_loop(0, ROWS, step, 0)
 
-    def home_to(k, part, send, recv):
-        return pltpu.make_async_remote_copy(
-            src_ref=rows.at[c, part], dst_ref=cols.at[q, part], send_sem=send.at[k],
-            recv_sem=recv.at[q], device_id=(k, user(k)), device_id_type=MESH,
-        )
-
-    def homes_arrived(buf, part, send, recv):
+    y_low = (c // 4) % 2
+    partner = c + 4 - 8 * y_low
+    near_row = (x_lo + y_low) % 2
+
+    def to_level(n, part, send, recv):
+        slot = c if n < 3 else partner
+        return pltpu.make_async_remote_copy(
+            src_ref=rows.at[slot, part], dst_ref=levels.at[n, part], send_sem=send.at[n],
+            recv_sem=recv.at[n], device_id=((z + 3 - n % 3) % 4 * 2 + x_lo, c),
+            device_id_type=MESH,
+        )
+
+    def at_level(n, part, send, recv):
+        return pltpu.make_async_remote_copy(
+            src_ref=levels.at[n, part], dst_ref=levels.at[n, part], send_sem=send.at[n],
+            recv_sem=recv.at[n], device_id=(r, twin(c)), device_id_type=MESH,
+        )
+
+    def to_user(n, part, send, recv):
+        away = n % 4
+        slot = (c if n < 4 else partner) % ROWS
+        block = (c if n < 4 else partner)
+        src = rows.at[block, part] if away == 0 else levels.at[away - 1 + 3 * (n // 4), part]
+        there = base + 4 * y_low + 2 * (away % 2) + away // 2
+        mine = jnp.logical_and(y_low == 0, there == c)
+        copy = pltpu.make_async_remote_copy(
+            src_ref=src, dst_ref=cols.at[slot, part], send_sem=send.at[n],
+            recv_sem=recv.at[slot], device_id=(2 * z + near_row, there), device_id_type=MESH,
+        )
+        return mine, src, slot, copy
+
+    def pass_to_user(n, part, send, recv):
+        mine, src, slot, copy = to_user(n, part, send, recv)
+
+        @pl.when(jnp.logical_not(mine))
+        def _():
+            copy.start()
+
+        @pl.when(mine)
+        def _():
+            cols[slot, part] = src[...]
+
+    def passed_to_user(n, part, send, recv):
+        mine, src, slot, copy = to_user(n, part, send, recv)
+
+        @pl.when(jnp.logical_not(mine))
+        def _():
+            copy.wait_send()
+
+    def spread(n0, part, l_send, l_recv, send, recv):
+        for away in (0, 1, 3, 2):
+            if away:
+                at_level(away - 1 + 3 * n0, part, l_send, l_recv).wait_recv()
+            pass_to_user(away + 4 * n0, part, send, recv)
+
+    def homes_arrived(buf, part, send, recv, kept):
         def step(k, carry):
-            @pl.when(jnp.logical_not(jnp.logical_and(same, k == q)))
+            @pl.when(jnp.logical_not(kept(k)))
             def _():
                 pltpu.make_async_remote_copy(
                     src_ref=buf.at[k, part], dst_ref=buf.at[k, part], send_sem=send.at[k],
@@ -207,18 +274,22 @@
 
     m_mine, m_relayed = row_copies(rows, M, rm_send, rm_recv)
     s_mine, s_relayed = row_copies(rows, S, rs_send, rs_recv)
-    m_mine[0].start()
-    users_each(lambda k: home_to(k, M, cm_send, cm_recv).start())
-    for copy in m_mine[1:]:
+    for copy in m_mine:
         copy.start()
-    s_mine[0].start()
-    users_each(lambda k: home_to(k, S, cs_send, cs_recv).start())
-    for copy in s_mine[1:]:
+    for n in range(3):
+        to_level(n, M, lm_send, lm_recv).start()
+    row_arrival(rows, partner, M, rm_send, rm_recv).wait_recv()
+    for n in range(3, 6):
+        to_level(n, M, lm_send, lm_recv).start()
+    row_arrival(rows, across(c), M, rm_send, rm_recv).wait_recv()
+    for copy in m_relayed:
         copy.start()
-
-    @pl.when(same)
-    def _():
-        cols[q] = rows[c]
+    spread(0, M, lm_send, lm_recv, cm_send, cm_recv)
+    spread(1, M, lm_send, lm_recv, cm_send, cm_recv)
+    for copy in s_mine:
+        copy.start()
+    for n in range(3):
+        to_level(n, S, ls_send, ls_recv).start()
 
     fetches[5].wait()
 
@@ -246,10 +317,7 @@
         hi, lo = halves(values)
         xs[v * 64 : v * 64 + 64, :] = jnp.concatenate([hi, lo], axis=0).astype(bf16)
 
-    row_arrival(rows, across(c), M, rm_send, rm_recv).wait_recv()
-    for copy in m_relayed:
-        copy.start()
-    homes_arrived(cols, M, cm_send, cm_recv)
+    homes_arrived(cols, M, cm_send, cm_recv, lambda k: jnp.logical_and(y_low == 0, k % 4 == q % 4))
     for v in range(ROWS):
         turned = jnp.concatenate([cols[v, EMB : 2 * EMB, :], -cols[v, 0:EMB, :]], axis=0)
         hi, lo = halves(turned)
@@ -271,7 +339,7 @@
     def score_step(t, carry):
         g = order(t)
 
-        @pl.when(jnp.logical_or(t % 2 == 1, t >= 4))
+        @pl.when(jnp.logical_or(t % 2 == 1, jnp.logical_and(t >= 4, g != partner)))
         def _():
             row_arrival(rows, g, M, rm_send, rm_recv).wait_recv()
 
@@ -281,6 +349,9 @@
 
         @pl.when(t == 4)
         def _():
+            row_arrival(rows, partner, S, rs_send, rs_recv).wait_recv()
+            for n in range(3, 6):
+                to_level(n, S, ls_send, ls_recv).start()
             row_arrival(rows, across(c), S, rs_send, rs_recv).wait_recv()
             for copy in s_relayed:
                 copy.start()
@@ -308,36 +379,70 @@
         f_part[g, FEAT:PART, :] = jnp.broadcast_to(sums, (8, B))
         return carry
 
-    lax.fori_loop(0, COLS, score_step, 0)
-    homes_arrived(cols, S, cs_send, cs_recv)
+    lax.fori_loop(0, SPREAD_AT, score_step, 0)
+    spread(0, S, ls_send, ls_recv, cs_send, cs_recv)
+    spread(1, S, ls_send, ls_recv, cs_send, cs_recv)
+    lax.fori_loop(SPREAD_AT, COLS, score_step, 0)
+    homes_arrived(cols, S, cs_send, cs_recv, lambda k: jnp.logical_and(y_low == 0, k % 4 == q % 4))
     for v in range(ROWS):
         put_columns(cols[v, 2 * EMB : ALL, :], v)
 
-    def first_step(t, carry):
-        g = order((t + 1) % COLS)
-
-        @pl.when(jnp.logical_and(t % 2 == 0, t >= 4))
-        def _():
-            row_arrival(rows, order(t), S, rs_send, rs_recv).wait_recv()
-            to_twin(t // 2, rows, S, rs_send, rs_recv).start()
-
-        f_part[g, 0:FEAT, :] = forward(g)
-
-        @pl.when(t < COLS - 1)
-        def _():
-            to_row(g, f_part.at[g], f_got, f_send, f_recv).start()
-
-        return carry
-
-    lax.fori_loop(0, COLS, first_step, 0)
-
-    def backward(first, last, rows_of, ready, with_degree):
-        if first == 0:
-            acc[...] = jnp.zeros_like(acc)
-
-        def step(t, carry):
-            g = order(t)
-            ready(t, g)
+    def pair_sum(g, part, pair, send, recv):
+        return pltpu.make_async_remote_copy(
+            src_ref=part.at[g], dst_ref=pair.at[g], send_sem=send.at[g], recv_sem=recv.at[g],
+            device_id=(r, twin(c)), device_id_type=MESH,
+        )
+
+    def forward_hop(part, pair, got, p_send, p_recv, send, recv, before):
+        def for_twin(h, carry):
+            before(h)
+            blocks = [order(2 * (h * STEP + n) + 1) for n in range(STEP)]
+            sums = [forward(g) for g in blocks]
+            for g, total in zip(blocks, sums):
+                part[g, 0:FEAT, :] = total
+            for g in blocks:
+                pair_sum(g, part, pair, p_send, p_recv).start()
+            return carry
+
+        def for_others(h, carry):
+            before(h + ROWS // STEP)
+            late = [(h * STEP + n + 1) % ROWS for n in range(STEP)]
+            blocks = [order(2 * i) for i in late]
+            sums = [forward(g) for g in blocks]
+            for g, total in zip(blocks, sums):
+                part[g, 0:FEAT, :] = total
+            for g, i in zip(blocks, late):
+                pair_sum(g, part, pair, p_send, p_recv).wait_recv()
+                part[g] = part[g] + pair[g]
+
+                @pl.when(i > 0)
+                def _():
+                    to_row(g, part.at[g], got, send, recv).start()
+
+            return carry
+
+        lax.fori_loop(0, ROWS // STEP, for_twin, 0)
+        lax.fori_loop(0, ROWS // STEP, for_others, 0)
+
+    def signals_on(h):
+        for n in range(0, STEP, 2):
+            t = h * STEP + n
+
+            @pl.when(t >= 4)
+            def _():
+                @pl.when(order(t) != partner)
+                def _():
+                    row_arrival(rows, order(t), S, rs_send, rs_recv).wait_recv()
+
+                to_twin(t // 2, rows, S, rs_send, rs_recv).start()
+
+    forward_hop(f_part, f_pair, f_got, p_send, p_recv, f_send, f_recv, signals_on)
+
+    def backward(rows_of, ready, with_degree):
+        acc[...] = jnp.zeros_like(acc)
+        depth = 528 if with_degree else 512
+
+        def fill(g, n):
             x = rows_of(g)
             for j in range(SLOTS):
                 window = idx[g, j : j + 1, :] >> 8
@@ -345,22 +450,32 @@
                 hi, lo = halves(x * value)
                 both = jnp.concatenate([hi, lo], axis=0)
                 for v in range(ROWS):
-                    st[v * 64 : v * 64 + 64, j * B : (j + 1) * B] = jnp.where(
+                    st[n, v * 64 : v * 64 + 64, j * B : (j + 1) * B] = jnp.where(
                         window == v, both, 0.0
                     ).astype(bf16)
                 if with_degree:
                     hi, lo = halves(value)
                     mine = lax.broadcasted_iota(i32, (8, B), 0) == window
-                    st[512:528, j * B : (j + 1) * B] = jnp.concatenate(
+                    st[n, 512:528, j * B : (j + 1) * B] = jnp.concatenate(
                         [jnp.where(mine, hi, 0.0), jnp.where(mine, lo, 0.0)], axis=0
                     ).astype(bf16)
-            depth = 528 if with_degree else 512
-            acc[0:depth, :] += lax.dot_general(
-                st[0:depth, :], hot[g], (((1,), (1,)), ((), ())), preferred_element_type=f32
-            )
+
+        def step(h, carry):
+            blocks = [order(h * STEP + n) for n in range(STEP)]
+            for n, g in enumerate(blocks):
+                ready(h * STEP + n, g)
+            for n, g in enumerate(blocks):
+                fill(g, n)
+            total = acc[0:depth, :]
+            for n, g in enumerate(blocks):
+                total = total + lax.dot_general(
+                    st[n, 0:depth, :], hot[g], (((1,), (1,)), ((), ())),
+                    preferred_element_type=f32,
+                )
+            acc[0:depth, :] = total
             return carry
 
-        lax.fori_loop(first, last, step, 0)
+        lax.fori_loop(0, COLS // STEP, step, 0)
 
     def keep_backward(part, with_degree):
         for v in range(ROWS):
@@ -385,12 +500,12 @@
             got[r] = part[q]
 
     def add_forward(part, got, send, recv):
-        def step(i, total):
-            k = (c + COLS - i) % COLS
+        def step(n, total):
+            k = (c + 2 * n) % COLS
             arrival(got, k, send, recv).wait_recv()
             return total + got[k]
 
-        return lax.fori_loop(1, COLS, step, part[c])
+        return lax.fori_loop(1, ROWS, step, part[c])
 
     def add_backward(got, send, recv):
         def step(k, total):
@@ -408,7 +523,9 @@
             row_arrival(rows, g, S, rs_send, rs_recv).wait_recv()
 
     own_signal = lambda g: rows[g, 2 * EMB : ALL, :]
-    backward(0, HALF1, own_signal, signal_ready, True)
+    backward(own_signal, signal_ready, True)
+    keep_backward(b_part, True)
+    give_back(b_part, b_got, b_send, b_recv)
 
     own = rows[c, 2 * EMB : ALL, :]
     summed = add_forward(f_part, f_got, f_send, f_recv)
@@ -416,54 +533,37 @@
     f_home[...] = KEEP * own + (summed[:FEAT] + own) * f_scale
     share_with_users(f_home, colx, c2_send, c2_recv)
 
-    backward(HALF1, COLS, own_signal, signal_ready, True)
-    keep_backward(b_part, True)
-    give_back(b_part, b_got, b_send, b_recv)
-
-    homes_arrived(colx, pl.ds(0, FEAT), c2_send, c2_recv)
-    for v in range(ROWS):
-        put_columns(colx[v], v)
-
-    def second_step(t, carry):
-        g = order(t + 1)
-        f_part2[g] = forward(g)
-        to_row(g, f_part2.at[g], f_got2, f2_send, f2_recv).start()
-        return carry
-
-    lax.fori_loop(0, HALF2, second_step, 0)
-
     summed = add_backward(b_got, b_send, b_recv)
     b_scale = GO / (1.0 + summed[FEAT : FEAT + 1])
     rowx[c] = KEEP * own + (summed[:FEAT] + own) * b_scale
     A = pl.ds(0, FEAT)
-    x_mine, x_relayed = row_copies(rowx, A, r2_send, r2_recv)
-    for copy in x_mine:
-        copy.start()
-
-    def relay(t):
-        @pl.when(t == HALF2 + 2)
-        def _():
-            row_arrival(rowx, across(c), A, r2_send, r2_recv).wait_recv()
-            for copy in x_relayed:
-                copy.start()
-
-    def second_late(t, carry):
-        relay(t)
-        return second_step(t, carry)
-
-    lax.fori_loop(HALF2, COLS - 1, second_late, 0)
-    f_part2[c] = forward(c)
+
+    def to_chip(n):
+        return pass_on((c + 2 * n) % COLS, rowx, c, rowx, A, n, r2_send, r2_recv)
+
+    def on_to_twin(n):
+        return pass_on(twin(c), rowx, (c + 2 * n) % COLS, rowx, A, ROWS + n, r2_send, r2_recv)
+
+    for n in range(1, ROWS):
+        to_chip(n).start()
+    on_to_twin(0).start()
+
+    homes_arrived(colx, pl.ds(0, FEAT), c2_send, c2_recv, lambda k: jnp.logical_and(same, k == q))
+    for v in range(ROWS):
+        put_columns(colx[v], v)
+
+    forward_hop(f_part2, f_pair2, f_got2, p2_send, p2_recv, f2_send, f2_recv, lambda h: None)
+
+    for n in range(1, ROWS):
+        row_arrival(rowx, (c + 2 * n) % COLS, A, r2_send, r2_recv).wait_recv()
+        on_to_twin(n).start()
 
     def ready(t, g):
-        @pl.when(jnp.logical_or(t % 2 == 1, t >= 4))
+        @pl.when(t % 2 == 1)
         def _():
             row_arrival(rowx, g, A, r2_send, r2_recv).wait_recv()
 
-        @pl.when(jnp.logical_and(t % 2 == 0, t >= 4))
-        def _():
-            to_twin(t // 2, rowx, A, r2_send, r2_recv).start()
-
-    backward(0, COLS, lambda g: rowx[g], ready, False)
+    backward(lambda g: rowx[g], ready, False)
     keep_backward(b_part2, False)
     give_back(b_part2, b_got2, b2_send, b2_recv)
 
@@ -472,18 +572,20 @@
     first = f_home[...]
     summed = add_forward(f_part2, f_got2, f2_send, f2_recv)
     second = KEEP * own + (summed + first) * f_scale
-    mixed = transposed_dot(wf[...], jnp.concatenate([own, first, second], axis=0))
+    mixed = full_dot(wf[...], jnp.concatenate([own, first, second], axis=0))
     first = rowx[c]
     summed = add_backward(b_got2, b2_send, b2_recv)
     second = KEEP * own + (summed + first) * b_scale
-    out[...] = mixed + transposed_dot(wb[...], jnp.concatenate([own, first, second], axis=0))
-
-    def sent(k):
-        home_to(k, M, cm_send, cm_recv).wait_send()
-        home_to(k, S, cs_send, cs_recv).wait_send()
-        to_users(k, f_home, colx, c2_send, c2_recv).wait_send()
-
-    users_each(sent)
+    out[...] = mixed + full_dot(wb[...], jnp.concatenate([own, first, second], axis=0))
+
+    users_each(lambda k: to_users(k, f_home, colx, c2_send, c2_recv).wait_send())
+
+    for n in range(6):
+        to_level(n, M, lm_send, lm_recv).wait_send()
+        to_level(n, S, ls_send, ls_recv).wait_send()
+    for n in range(8):
+        passed_to_user(n, M, cm_send, cm_recv)
+        passed_to_user(n, S, cs_send, cs_recv)
 
     def sent_to_homes(k, carry):
         @pl.when(jnp.logical_not(jnp.logical_and(same, k == q)))
@@ -493,21 +595,29 @@
 
         return carry
 
-    def sent_to_row(i, carry):
-        k = (c + i) % COLS
+    def sent_to_row(n, carry):
+        k = (c + 2 * n) % COLS
         to_row(k, f_part.at[k], f_got, f_send, f_recv).wait_send()
         to_row(k, f_part2.at[k], f_got2, f2_send, f2_recv).wait_send()
-        return carry
-
+        to_chip(n).wait_send()
+        return carry
+
+    def sent_to_pair(n, carry):
+        k = (twin(c) + 2 * n) % COLS
+        pair_sum(k, f_part, f_pair, p_send, p_recv).wait_send()
+        pair_sum(k, f_part2, f_pair2, p2_send, p2_recv).wait_send()
+        on_to_twin(n).wait_send()
+        return carry
+
+    lax.fori_loop(0, ROWS, sent_to_pair, 0)
     lax.fori_loop(0, ROWS, sent_to_homes, 0)
-    lax.fori_loop(1, COLS, sent_to_row, 0)
-    for copy in m_mine + m_relayed + s_mine + s_relayed + x_mine + x_relayed:
+    lax.fori_loop(1, ROWS, sent_to_row, 0)
+    for copy in m_mine + m_relayed + s_mine + s_relayed:
         copy.wait_send()
 
     def sent_to_twin(i, carry):
         to_twin(i, rows, M, rm_send, rm_recv).wait_send()
         to_twin(i, rows, S, rs_send, rs_recv).wait_send()
-        to_twin(i, rowx, A, r2_send, r2_recv).wait_send()
         return carry
 
     lax.fori_loop(2, ROWS, sent_to_twin, 0)
@@ -519,26 +629,29 @@
     dma = pltpu.SemaphoreType.DMA
     scratch = [
         vmem((EMB, B), f32), vmem((EMB, B), f32), vmem((EMB, EMB), f32), vmem((EMB, EMB), f32),
-        vmem((keep_count, COLS * B), i32), vmem((3 * FEAT, FEAT), f32), vmem((3 * FEAT, FEAT), f32),
+        vmem((keep_count, COLS * B), i32), vmem((FEAT, 3 * FEAT), f32), vmem((FEAT, 3 * FEAT), f32),
         vmem((COLS, ALL, B), f32),
         vmem((ROWS, ALL, B), f32),
+        vmem((6, ALL, B), f32),
         vmem((ROWS * B, 6 * EMB), bf16),
         vmem((6 * EMB, B), bf16),
         vmem((512, B), bf16),
-        vmem((528, SLOTS * B), bf16),
+        vmem((STEP, 528, SLOTS * B), bf16),
         vmem((COLS, B, SLOTS * B), bf16),
         vmem((COLS, 8, B), i32),
         vmem((COLS, 8, B), f32),
         vmem((528, B), f32),
         vmem((COLS, PART, B), f32), vmem((COLS, PART, B), f32),
+        vmem((COLS, PART, B), f32),
         vmem((ROWS, PART, B), f32), vmem((ROWS, PART, B), f32),
         vmem((FEAT, B), f32),
         vmem((ROWS, FEAT, B), f32), vmem((COLS, FEAT, B), f32),
         vmem((COLS, FEAT, B), f32), vmem((COLS, FEAT, B), f32),
+        vmem((COLS, FEAT, B), f32),
         vmem((ROWS, FEAT, B), f32), vmem((ROWS, FEAT, B), f32),
         dma((8,)),
     ]
-    for count in (ROWS, ROWS, COLS, COLS, COLS, ROWS, ROWS, COLS, COLS, ROWS):
+    for count in (6, 6, ROWS, ROWS, COLS, COLS, COLS, ROWS, ROWS, COLS, COLS, ROWS, COLS, COLS):
         scratch += [dma((count,)), dma((count,))]
     return pl.pallas_call(
         kernel,
@@ -547,10 +660,10 @@
         out_specs=pl.BlockSpec(memory_space=pltpu.VMEM),
         scratch_shapes=scratch,
         compiler_params=pltpu.CompilerParams(
-            collective_id=0, has_side_effects=True, vmem_limit_bytes=48 * 1024 * 1024
+            collective_id=0, has_side_effects=True, vmem_limit_bytes=VMEM_BYTES
         ),
         name="graph_layer",
-    )(*args)
+    )(*args[:6], args[6].T, args[7].T)
 
 
 def solution(mesh):

time: 93.7 us -> 80 us (0.85)
  Pallas kernels: 88.2 us -> 78.4 us
  local copies, waits for them, and re-layouts: 4.7 us -> 1.38 us
    pallas_call x1, Pallas kernels: 88.2 us -> 78.4 us  [per_device(): pl.pallas_call(kernel, out_shape=jax.ShapeDtypeStruct((FEAT, B), f32), in...]
    unnamed x15 -> x1, local copies, waits for them, and re-layouts: 4.7 us -> 1.38 us
where the time goes in v3:
time: 80 us; the launch traced here: 79.8 us
  Pallas kernels  78.4 us (98%)
  local copies, waits for them, and re-layouts  1.38 us (2%)
    pallas_call x1, Pallas kernels, per_device(): pl.pallas_call(kernel, out_shape=jax.ShapeDtypeStruct((FEAT, B), f32), in...  78.4 us

profile of v3, /device:TPU:1, one launch (start us, length us, event | category | flops | bytes accessed | tf_op | source)
XLA Modules:
  0.0 79.8 jit_solution(17850135329690461525)
XLA Ops:
  0.0 78.4 %graph_layer.1 = f32[32,256]{1,0:T(8,128)} custom-call(f32[40,256]{1,0:T(8,128)} %emb_first.1, f32[40,256]{1,0:T(8,128)} %emb_second.1, f32[32,256]{1,0:T(8,128)} %signal.1, f32[40,40]{1,0:T(8,128)} %theta_first.1, f32[40,40]{1,0:T(8,128)} %theta_second.1, s32[20,4096]{1,0:T(8,128)} %neighbors.1, f32[32,96]{1,0:T(8,128)} %bitcast.2, f32[32,96]{1,0:T(8,128)} %bitcast.3), custom_call_target="tpu_custom_call" | custom-call | tf_op jit(solution)/shard_map/graph_layer/pallas_call | solution.py:656
  78.4 1.4 %copy.10 = f32[32,256]{1,0:T(8,128)} copy(f32[32,256]{1,0:T(8,128)} %graph_layer.1) | data formatting | bytes 65536

commit v4 on v3

--- a/solution.py
+++ b/solution.py
@@ -19,7 +19,6 @@
 FEAT = 32
 ALL = 2 * EMB + FEAT
 VMEM_BYTES = 60 * 1024 * 1024
-SPREAD_AT = 8
 STEP = 4
 PART = FEAT + 8
 
@@ -43,10 +42,9 @@
     emb_first, emb_second, signal, theta_first, theta_second, neighbors, w_forward, w_backward,
     out,
     emb1, emb2, theta1, theta2, near, wf, wb,
-    rows, cols, levels, right, left, xs, st, hot, idx, weight, acc,
+    rows, cols, right, left, xs, st, hot, idx, weight, acc,
     f_part, f_pair, f_got, b_part, b_got, f_home, colx, rowx, f_part2, f_pair2, f_got2, b_part2, b_got2,
-    in_sem, lm_send, lm_recv, ls_send, ls_recv, cm_send, cm_recv, cs_send, cs_recv,
-    rm_send, rm_recv, rs_send, rs_recv,
+    in_sem, cm_send, cm_recv, cs_send, cs_recv, rm_send, rm_recv, rs_send, rs_recv,
     f_send, f_recv, b_send, b_recv, c2_send, c2_recv, r2_send, r2_recv,
     f2_send, f2_recv, b2_send, b2_recv, p_send, p_recv, p2_send, p2_recv,
 ):
@@ -84,18 +82,6 @@
         return carry
 
     lax.fori_loop(1, COLS, greet, 0)
-    for n in range(1, 4):
-        pl.semaphore_signal(
-            barrier, inc=1, device_id=((z + n) % 4 * 2 + x_lo, c), device_id_type=MESH
-        )
-
-    @pl.when((c // 4) % 2 == 1)
-    def _():
-        for n in range(4):
-            pl.semaphore_signal(
-                barrier, inc=1, device_id=(2 * z + 1 - x_lo, c - c % 4 + n), device_id_type=MESH
-            )
-
     lax.fori_loop(0, ROWS, greet_columns, 0)
 
     fetches = [
@@ -115,7 +101,7 @@
     rows[c, 0:EMB, :] = jnp.tanh(3.0 * transposed_dot(theta1[...], emb1[...]))
     rows[c, EMB : 2 * EMB, :] = jnp.tanh(3.0 * transposed_dot(theta2[...], emb2[...]))
 
-    pl.semaphore_wait(barrier, COLS - 1 + 2 * (ROWS - 1) + 2 * others + 3 + 4 * ((c // 4) % 2))
+    pl.semaphore_wait(barrier, COLS - 1 + 2 * (ROWS - 1) + 2 * others)
 
     def to_users(k, src, dst, send, recv):
         return pltpu.make_async_remote_copy(
@@ -189,60 +175,33 @@
     partner = c + 4 - 8 * y_low
     near_row = (x_lo + y_low) % 2
 
-    def to_level(n, part, send, recv):
-        slot = c if n < 3 else partner
-        return pltpu.make_async_remote_copy(
-            src_ref=rows.at[slot, part], dst_ref=levels.at[n, part], send_sem=send.at[n],
-            recv_sem=recv.at[n], device_id=((z + 3 - n % 3) % 4 * 2 + x_lo, c),
-            device_id_type=MESH,
-        )
-
-    def at_level(n, part, send, recv):
-        return pltpu.make_async_remote_copy(
-            src_ref=levels.at[n, part], dst_ref=levels.at[n, part], send_sem=send.at[n],
-            recv_sem=recv.at[n], device_id=(r, twin(c)), device_id_type=MESH,
-        )
-
-    def to_user(n, part, send, recv):
-        away = n % 4
-        slot = (c if n < 4 else partner) % ROWS
-        block = (c if n < 4 else partner)
-        src = rows.at[block, part] if away == 0 else levels.at[away - 1 + 3 * (n // 4), part]
-        there = base + 4 * y_low + 2 * (away % 2) + away // 2
-        mine = jnp.logical_and(y_low == 0, there == c)
-        copy = pltpu.make_async_remote_copy(
-            src_ref=src, dst_ref=cols.at[slot, part], send_sem=send.at[n],
-            recv_sem=recv.at[slot], device_id=(2 * z + near_row, there), device_id_type=MESH,
-        )
-        return mine, src, slot, copy
-
-    def pass_to_user(n, part, send, recv):
-        mine, src, slot, copy = to_user(n, part, send, recv)
-
-        @pl.when(jnp.logical_not(mine))
-        def _():
-            copy.start()
-
-        @pl.when(mine)
-        def _():
-            cols[slot, part] = src[...]
-
-    def passed_to_user(n, part, send, recv):
-        mine, src, slot, copy = to_user(n, part, send, recv)
-
-        @pl.when(jnp.logical_not(mine))
-        def _():
-            copy.wait_send()
-
-    def spread(n0, part, l_send, l_recv, send, recv):
-        for away in (0, 1, 3, 2):
-            if away:
-                at_level(away - 1 + 3 * n0, part, l_send, l_recv).wait_recv()
-            pass_to_user(away + 4 * n0, part, send, recv)
+    def home_to(i, slot, part, send, recv):
+        k = 2 * i + near_row
+        n = i + 4 * (jnp.where(slot == c, 0, 1).astype(i32))
+        return pltpu.make_async_remote_copy(
+            src_ref=rows.at[slot, part], dst_ref=cols.at[slot % ROWS, part], send_sem=send.at[n],
+            recv_sem=recv.at[slot % ROWS], device_id=(k, user(k)), device_id_type=MESH,
+        )
+
+    def homes_each(slot, do):
+        def step(j, carry):
+            i = (z + j) % 4
+
+            @pl.when(jnp.logical_not(own_user(i)))
+            def _():
+                do(i, slot)
+
+            return carry
+
+        lax.fori_loop(0, 4, step, 0)
+
+    def own_user(i):
+        k = 2 * i + near_row
+        return jnp.logical_and(k == r, user(k) == c)
 
     def homes_arrived(buf, part, send, recv, kept):
         def step(k, carry):
-            @pl.when(jnp.logical_not(kept(k)))
+            @pl.when(jnp.logical_not(jnp.logical_and(same, kept(k))))
             def _():
                 pltpu.make_async_remote_copy(
                     src_ref=buf.at[k, part], dst_ref=buf.at[k, part], send_sem=send.at[k],
@@ -274,22 +233,31 @@
 
     m_mine, m_relayed = row_copies(rows, M, rm_send, rm_recv)
     s_mine, s_relayed = row_copies(rows, S, rs_send, rs_recv)
-    for copy in m_mine:
+    for copy in (m_mine[1], m_mine[2], m_mine[0]):
         copy.start()
-    for n in range(3):
-        to_level(n, M, lm_send, lm_recv).start()
-    row_arrival(rows, partner, M, rm_send, rm_recv).wait_recv()
-    for n in range(3, 6):
-        to_level(n, M, lm_send, lm_recv).start()
+    homes_each(c, lambda i, slot: home_to(i, slot, M, cm_send, cm_recv).start())
+    for copy in m_mine[3:]:
+        copy.start()
+
+    @pl.when(same)
+    def _():
+        cols[q] = rows[c]
+
+    def partner_block(part, buf_send, buf_recv, send, recv):
+        row_arrival(rows, partner, part, buf_send, buf_recv).wait_recv()
+        homes_each(partner, lambda i, slot: home_to(i, slot, part, send, recv).start())
+
+        @pl.when(same)
+        def _():
+            cols[partner % ROWS, part] = rows[partner, part]
+
+    partner_block(M, rm_send, rm_recv, cm_send, cm_recv)
     row_arrival(rows, across(c), M, rm_send, rm_recv).wait_recv()
     for copy in m_relayed:
         copy.start()
-    spread(0, M, lm_send, lm_recv, cm_send, cm_recv)
-    spread(1, M, lm_send, lm_recv, cm_send, cm_recv)
     for copy in s_mine:
         copy.start()
-    for n in range(3):
-        to_level(n, S, ls_send, ls_recv).start()
+    homes_each(c, lambda i, slot: home_to(i, slot, S, cs_send, cs_recv).start())
 
     fetches[5].wait()
 
@@ -317,7 +285,7 @@
         hi, lo = halves(values)
         xs[v * 64 : v * 64 + 64, :] = jnp.concatenate([hi, lo], axis=0).astype(bf16)
 
-    homes_arrived(cols, M, cm_send, cm_recv, lambda k: jnp.logical_and(y_low == 0, k % 4 == q % 4))
+    homes_arrived(cols, M, cm_send, cm_recv, lambda k: k % 4 == 0)
     for v in range(ROWS):
         turned = jnp.concatenate([cols[v, EMB : 2 * EMB, :], -cols[v, 0:EMB, :]], axis=0)
         hi, lo = halves(turned)
@@ -349,9 +317,7 @@
 
         @pl.when(t == 4)
         def _():
-            row_arrival(rows, partner, S, rs_send, rs_recv).wait_recv()
-            for n in range(3, 6):
-                to_level(n, S, ls_send, ls_recv).start()
+            partner_block(S, rs_send, rs_recv, cs_send, cs_recv)
             row_arrival(rows, across(c), S, rs_send, rs_recv).wait_recv()
             for copy in s_relayed:
                 copy.start()
@@ -379,11 +345,8 @@
         f_part[g, FEAT:PART, :] = jnp.broadcast_to(sums, (8, B))
         return carry
 
-    lax.fori_loop(0, SPREAD_AT, score_step, 0)
-    spread(0, S, ls_send, ls_recv, cs_send, cs_recv)
-    spread(1, S, ls_send, ls_recv, cs_send, cs_recv)
-    lax.fori_loop(SPREAD_AT, COLS, score_step, 0)
-    homes_arrived(cols, S, cs_send, cs_recv, lambda k: jnp.logical_and(y_low == 0, k % 4 == q % 4))
+    lax.fori_loop(0, COLS, score_step, 0)
+    homes_arrived(cols, S, cs_send, cs_recv, lambda k: k % 4 == 0)
     for v in range(ROWS):
         put_columns(cols[v, 2 * EMB : ALL, :], v)
 
@@ -548,7 +511,7 @@
         to_chip(n).start()
     on_to_twin(0).start()
 
-    homes_arrived(colx, pl.ds(0, FEAT), c2_send, c2_recv, lambda k: jnp.logical_and(same, k == q))
+    homes_arrived(colx, pl.ds(0, FEAT), c2_send, c2_recv, lambda k: k == q)
     for v in range(ROWS):
         put_columns(colx[v], v)
 
@@ -580,12 +543,12 @@
 
     users_each(lambda k: to_users(k, f_home, colx, c2_send, c2_recv).wait_send())
 
-    for n in range(6):
-        to_level(n, M, lm_send, lm_recv).wait_send()
-        to_level(n, S, ls_send, ls_recv).wait_send()
-    for n in range(8):
-        passed_to_user(n, M, cm_send, cm_recv)
-        passed_to_user(n, S, cs_send, cs_recv)
+    def sent(i, slot):
+        home_to(i, slot, M, cm_send, cm_recv).wait_send()
+        home_to(i, slot, S, cs_send, cs_recv).wait_send()
+
+    homes_each(c, sent)
+    homes_each(partner, sent)
 
     def sent_to_homes(k, carry):
         @pl.when(jnp.logical_not(jnp.logical_and(same, k == q)))
@@ -632,7 +595,6 @@
         vmem((keep_count, COLS * B), i32), vmem((FEAT, 3 * FEAT), f32), vmem((FEAT, 3 * FEAT), f32),
         vmem((COLS, ALL, B), f32),
         vmem((ROWS, ALL, B), f32),
-        vmem((6, ALL, B), f32),
         vmem((ROWS * B, 6 * EMB), bf16),
         vmem((6 * EMB, B), bf16),
         vmem((512, B), bf16),
@@ -651,7 +613,7 @@
         vmem((ROWS, FEAT, B), f32), vmem((ROWS, FEAT, B), f32),
         dma((8,)),
     ]
-    for count in (6, 6, ROWS, ROWS, COLS, COLS, COLS, ROWS, ROWS, COLS, COLS, ROWS, COLS, COLS):
+    for count in (ROWS, ROWS, COLS, COLS, COLS, ROWS, ROWS, COLS, COLS, ROWS, COLS, COLS):
         scratch += [dma((count,)), dma((count,))]
     return pl.pallas_call(
         kernel,

time: 80 us -> 77.1 us (0.964)
  Pallas kernels: 78.4 us -> 75.4 us
    pallas_call x1, Pallas kernels: 78.4 us -> 75.4 us  [per_device(): pl.pallas_call(kernel, out_shape=jax.ShapeDtypeStruct((FEAT, B), f32), in...]
where the time goes in v4:
time: 77.1 us; the launch traced here: 76.8 us
  Pallas kernels  75.4 us (98%)
  local copies, waits for them, and re-layouts  1.38 us (2%)
    pallas_call x1, Pallas kernels, per_device(): pl.pallas_call(kernel, out_shape=jax.ShapeDtypeStruct((FEAT, B), f32), in...  75.4 us

profile of v4, /device:TPU:1, one launch (start us, length us, event | category | flops | bytes accessed | tf_op | source)
XLA Modules:
  0.0 76.8 jit_solution(5641790292919532321)
XLA Ops:
  0.0 75.4 %graph_layer.1 = f32[32,256]{1,0:T(8,128)} custom-call(f32[40,256]{1,0:T(8,128)} %emb_first.1, f32[40,256]{1,0:T(8,128)} %emb_second.1, f32[32,256]{1,0:T(8,128)} %signal.1, f32[40,40]{1,0:T(8,128)} %theta_first.1, f32[40,40]{1,0:T(8,128)} %theta_second.1, s32[20,4096]{1,0:T(8,128)} %neighbors.1, f32[32,96]{1,0:T(8,128)} %bitcast.2, f32[32,96]{1,0:T(8,128)} %bitcast.3), custom_call_target="tpu_custom_call" | custom-call | tf_op jit(solution)/shard_map/graph_layer/pallas_call | solution.py:618
  75.4 1.4 %copy.10 = f32[32,256]{1,0:T(8,128)} copy(f32[32,256]{1,0:T(8,128)} %graph_layer.1) | data formatting | bytes 65536

commit v5 on v4

--- a/solution.py
+++ b/solution.py
@@ -143,6 +143,9 @@
         slot = slot + (i % 2) * (2 - 4 * ((slot // 2) % 2))
         return slot + (t % 2) * (1 - 2 * (slot % 2))
 
+    def own_core_first(step):
+        return 2 * (step % ROWS) + step // ROWS
+
     M = pl.ds(0, 2 * EMB)
     S = pl.ds(2 * EMB, FEAT)
 
@@ -304,7 +307,8 @@
             total = total + weight[g, j : j + 1, :] * (part[:FEAT] + part[FEAT:])
         return total
 
-    def score_step(t, carry):
+    def score_step(step, carry):
+        t = own_core_first(step)
         g = order(t)
 
         @pl.when(jnp.logical_or(t % 2 == 1, jnp.logical_and(t >= 4, g != partner)))
@@ -424,9 +428,10 @@
                     ).astype(bf16)
 
         def step(h, carry):
-            blocks = [order(h * STEP + n) for n in range(STEP)]
-            for n, g in enumerate(blocks):
-                ready(h * STEP + n, g)
+            times = [own_core_first(h * STEP + n) for n in range(STEP)]
+            blocks = [order(t) for t in times]
+            for t, g in zip(times, blocks):
+                ready(t, g)
             for n, g in enumerate(blocks):
                 fill(g, n)
             total = acc[0:depth, :]

time: 77.1 us -> 74.8 us (0.970)
  Pallas kernels: 75.4 us -> 73.2 us
    pallas_call x1, Pallas kernels: 75.4 us -> 73.2 us  [per_device(): pl.pallas_call(kernel, out_shape=jax.ShapeDtypeStruct((FEAT, B), f32), in...]
where the time goes in v5:
time: 74.8 us; the launch traced here: 74.6 us
  Pallas kernels  73.2 us (98%)
  local copies, waits for them, and re-layouts  1.38 us (2%)
    pallas_call x1, Pallas kernels, per_device(): pl.pallas_call(kernel, out_shape=jax.ShapeDtypeStruct((FEAT, B), f32), in...  73.2 us

profile of v5, /device:TPU:1, one launch (start us, length us, event | category | flops | bytes accessed | tf_op | source)
XLA Modules:
  0.0 74.6 jit_solution(15692317804704632598)
XLA Ops:
  0.0 73.2 %graph_layer.1 = f32[32,256]{1,0:T(8,128)} custom-call(f32[40,256]{1,0:T(8,128)} %emb_first.1, f32[40,256]{1,0:T(8,128)} %emb_second.1, f32[32,256]{1,0:T(8,128)} %signal.1, f32[40,40]{1,0:T(8,128)} %theta_first.1, f32[40,40]{1,0:T(8,128)} %theta_second.1, s32[20,4096]{1,0:T(8,128)} %neighbors.1, f32[32,96]{1,0:T(8,128)} %bitcast.2, f32[32,96]{1,0:T(8,128)} %bitcast.3), custom_call_target="tpu_custom_call" | custom-call | tf_op jit(solution)/shard_map/graph_layer/pallas_call | solution.py:623
  73.2 1.4 %copy.10 = f32[32,256]{1,0:T(8,128)} copy(f32[32,256]{1,0:T(8,128)} %graph_layer.1) | data formatting | bytes 65536

commit v6 on v5

--- a/solution.py
+++ b/solution.py
@@ -535,6 +535,50 @@
     keep_backward(b_part2, False)
     give_back(b_part2, b_got2, b2_send, b2_recv)
 
+    users_each(lambda k: to_users(k, f_home, colx, c2_send, c2_recv).wait_send())
+
+    def sent(i, slot):
+        home_to(i, slot, M, cm_send, cm_recv).wait_send()
+        home_to(i, slot, S, cs_send, cs_recv).wait_send()
+
+    homes_each(c, sent)
+    homes_each(partner, sent)
+
+    def sent_to_homes(k, carry):
+        @pl.when(jnp.logical_not(jnp.logical_and(same, k == q)))
+        def _():
+            to_homes(k, b_part.at[k], b_got, b_send, b_recv).wait_send()
+            to_homes(k, b_part2.at[k], b_got2, b2_send, b2_recv).wait_send()
+
+        return carry
+
+    def sent_to_row(n, carry):
+        k = (c + 2 * n) % COLS
+        to_row(k, f_part.at[k], f_got, f_send, f_recv).wait_send()
+        to_row(k, f_part2.at[k], f_got2, f2_send, f2_recv).wait_send()
+        to_chip(n).wait_send()
+        return carry
+
+    def sent_to_pair(n, carry):
+        k = (twin(c) + 2 * n) % COLS
+        pair_sum(k, f_part, f_pair, p_send, p_recv).wait_send()
+        pair_sum(k, f_part2, f_pair2, p2_send, p2_recv).wait_send()
+        on_to_twin(n).wait_send()
+        return carry
+
+    lax.fori_loop(0, ROWS, sent_to_pair, 0)
+    lax.fori_loop(0, ROWS, sent_to_homes, 0)
+    lax.fori_loop(1, ROWS, sent_to_row, 0)
+    for copy in m_mine + m_relayed + s_mine + s_relayed:
+        copy.wait_send()
+
+    def sent_to_twin(i, carry):
+        to_twin(i, rows, M, rm_send, rm_recv).wait_send()
+        to_twin(i, rows, S, rs_send, rs_recv).wait_send()
+        return carry
+
+    lax.fori_loop(2, ROWS, sent_to_twin, 0)
+
     fetches[6].wait()
     fetches[7].wait()
     first = f_home[...]
@@ -545,50 +589,6 @@
     summed = add_backward(b_got2, b2_send, b2_recv)
     second = KEEP * own + (summed + first) * b_scale
     out[...] = mixed + full_dot(wb[...], jnp.concatenate([own, first, second], axis=0))
-
-    users_each(lambda k: to_users(k, f_home, colx, c2_send, c2_recv).wait_send())
-
-    def sent(i, slot):
-        home_to(i, slot, M, cm_send, cm_recv).wait_send()
-        home_to(i, slot, S, cs_send, cs_recv).wait_send()
-
-    homes_each(c, sent)
-    homes_each(partner, sent)
-
-    def sent_to_homes(k, carry):
-        @pl.when(jnp.logical_not(jnp.logical_and(same, k == q)))
-        def _():
-            to_homes(k, b_part.at[k], b_got, b_send, b_recv).wait_send()
-            to_homes(k, b_part2.at[k], b_got2, b2_send, b2_recv).wait_send()
-
-        return carry
-
-    def sent_to_row(n, carry):
-        k = (c + 2 * n) % COLS
-        to_row(k, f_part.at[k], f_got, f_send, f_recv).wait_send()
-        to_row(k, f_part2.at[k], f_got2, f2_send, f2_recv).wait_send()
-        to_chip(n).wait_send()
-        return carry
-
-    def sent_to_pair(n, carry):
-        k = (twin(c) + 2 * n) % COLS
-        pair_sum(k, f_part, f_pair, p_send, p_recv).wait_send()
-        pair_sum(k, f_part2, f_pair2, p2_send, p2_recv).wait_send()
-        on_to_twin(n).wait_send()
-        return carry
-
-    lax.fori_loop(0, ROWS, sent_to_pair, 0)
-    lax.fori_loop(0, ROWS, sent_to_homes, 0)
-    lax.fori_loop(1, ROWS, sent_to_row, 0)
-    for copy in m_mine + m_relayed + s_mine + s_relayed:
-        copy.wait_send()
-
-    def sent_to_twin(i, carry):
-        to_twin(i, rows, M, rm_send, rm_recv).wait_send()
-        to_twin(i, rows, S, rs_send, rs_recv).wait_send()
-        return carry
-
-    lax.fori_loop(2, ROWS, sent_to_twin, 0)
 
 
 def per_device(*args):

time: 74.8 us -> 74 us (0.989)
  Pallas kernels: 73.2 us -> 72.4 us
    pallas_call x1, Pallas kernels: 73.2 us -> 72.4 us  [per_device(): pl.pallas_call(kernel, out_shape=jax.ShapeDtypeStruct((FEAT, B), f32), in...]
where the time goes in v6:
time: 74 us; the launch traced here: 73.8 us
  Pallas kernels  72.4 us (98%)
  local copies, waits for them, and re-layouts  1.38 us (2%)
    pallas_call x1, Pallas kernels, per_device(): pl.pallas_call(kernel, out_shape=jax.ShapeDtypeStruct((FEAT, B), f32), in...  72.4 us

profile of v6, /device:TPU:1, one launch (start us, length us, event | category | flops | bytes accessed | tf_op | source)
XLA Modules:
  0.0 73.8 jit_solution(1268768980530614352)
XLA Ops:
  0.0 72.4 %graph_layer.1 = f32[32,256]{1,0:T(8,128)} custom-call(f32[40,256]{1,0:T(8,128)} %emb_first.1, f32[40,256]{1,0:T(8,128)} %emb_second.1, f32[32,256]{1,0:T(8,128)} %signal.1, f32[40,40]{1,0:T(8,128)} %theta_first.1, f32[40,40]{1,0:T(8,128)} %theta_second.1, s32[20,4096]{1,0:T(8,128)} %neighbors.1, f32[32,96]{1,0:T(8,128)} %bitcast.2, f32[32,96]{1,0:T(8,128)} %bitcast.3), custom_call_target="tpu_custom_call" | custom-call | tf_op jit(solution)/shard_map/graph_layer/pallas_call | solution.py:623
  72.5 1.4 %copy.10 = f32[32,256]{1,0:T(8,128)} copy(f32[32,256]{1,0:T(8,128)} %graph_layer.1) | data formatting | bytes 65536

commit v7 on v5

--- a/solution.py
+++ b/solution.py
@@ -541,11 +541,6 @@
     summed = add_forward(f_part2, f_got2, f2_send, f2_recv)
     second = KEEP * own + (summed + first) * f_scale
     mixed = full_dot(wf[...], jnp.concatenate([own, first, second], axis=0))
-    first = rowx[c]
-    summed = add_backward(b_got2, b2_send, b2_recv)
-    second = KEEP * own + (summed + first) * b_scale
-    out[...] = mixed + full_dot(wb[...], jnp.concatenate([own, first, second], axis=0))
-
     users_each(lambda k: to_users(k, f_home, colx, c2_send, c2_recv).wait_send())
 
     def sent(i, slot):
@@ -589,6 +584,12 @@
         return carry
 
     lax.fori_loop(2, ROWS, sent_to_twin, 0)
+
+    first = rowx[c]
+    mixed = mixed + full_dot(wb[:, 0 : 2 * FEAT], jnp.concatenate([own, first], axis=0))
+    summed = add_backward(b_got2, b2_send, b2_recv)
+    second = KEEP * own + (summed + first) * b_scale
+    out[...] = mixed + full_dot(wb[:, 2 * FEAT : 3 * FEAT], second)
 
 
 def per_device(*args):

time: 74.8 us -> 74 us (0.989)
    pallas_call x1, Pallas kernels: 73.2 us -> 72.5 us  [per_device(): pl.pallas_call(kernel, out_shape=jax.ShapeDtypeStruct((FEAT, B), f32), in...]
where the time goes in v7:
time: 74 us; the launch traced here: 73.9 us
  Pallas kernels  72.5 us (98%)
  local copies, waits for them, and re-layouts  1.38 us (2%)
    pallas_call x1, Pallas kernels, per_device(): pl.pallas_call(kernel, out_shape=jax.ShapeDtypeStruct((FEAT, B), f32), in...  72.5 us

profile of v7, /device:TPU:1, one launch (start us, length us, event | category | flops | bytes accessed | tf_op | source)
XLA Modules:
  0.0 73.9 jit_solution(840979977506718489)
XLA Ops:
  0.0 72.5 %graph_layer.1 = f32[32,256]{1,0:T(8,128)} custom-call(f32[40,256]{1,0:T(8,128)} %emb_first.1, f32[40,256]{1,0:T(8,128)} %emb_second.1, f32[32,256]{1,0:T(8,128)} %signal.1, f32[40,40]{1,0:T(8,128)} %theta_first.1, f32[40,40]{1,0:T(8,128)} %theta_second.1, s32[20,4096]{1,0:T(8,128)} %neighbors.1, f32[32,96]{1,0:T(8,128)} %bitcast.2, f32[32,96]{1,0:T(8,128)} %bitcast.3), custom_call_target="tpu_custom_call" | custom-call | tf_op jit(solution)/shard_map/graph_layer/pallas_call | solution.py:624
  72.5 1.4 %copy.10 = f32[32,256]{1,0:T(8,128)} copy(f32[32,256]{1,0:T(8,128)} %graph_layer.1) | data formatting | bytes 65536
